TPU v7x, 128 devices: a whole 4x4x4 slice. The times are simulated.
128 devices in a mesh: ctx: 16 (over x_lo, y, core), tp: 8 (over x_hi, z).
Axes of the slice: x: 4 (x_hi: 2, x_lo: 2; x = x_hi * 2 + x_lo), y: 4, z: 4, core: 2. Of those that a mesh axis runs over, the one named last changes fastest.
Arguments:
- activations: bfloat16 [4096, 8192], P('ctx', 'tp'), may hold values from -6 to 6
- proj_weight: bfloat16 [8192, 12288], P('tp'), may hold values from -0.0625 to 0.0625
- filter_taps: float32 [4096, 4096], P(None, ('ctx', 'tp')), may hold values from -0.09375 to 0.09375
- filter_blocks: int32 [4096], replicated, may hold values from 1 to 16, as said below
- skip_gain: float32 [4096], replicated, may hold values from 0.5 to 1.5
Outputs:
- mixed_out: bfloat16 [4096, 4096], P(None, ('ctx', 'tp'))
Inputs may be any that keep to these rules, and one draw needn't show every extreme that they name: `filter_blocks`: some channel has exactly 1 block and some channel has all 16 blocks.
All inputs are finite; a program needn't handle non-finite values.
Results may differ from a plain program's by a relative error of at most 0.025.
Values may be sent and summed in bfloat16 or wider, within the bound.
A program may use at most 128 MiB of HBM per device.

v0:
```python
import functools
import math

import jax
import jax.numpy as jnp
import ml_dtypes
import numpy as np
from jax import lax
from jax.experimental import pallas as pl
from jax.experimental.pallas import tpu as pltpu
from jax.sharding import PartitionSpec as P

BF = jnp.bfloat16
F32 = jnp.float32
OUTER = 32
INNER = 128
LENGTH = OUTER * INNER
SHIFT = 0.25

ROWS_Z = 144
LANES_Z = 2304


def flipped(index):
    return int(format(index, "05b")[::-1], 2)


def tables():
    at = np.arange(INNER)
    angle = 2.0 * math.pi * (at[:, None] * at[None, :] % INNER) / INNER
    cos, sin = np.cos(angle), np.sin(angle)
    forward = np.block([[cos, -sin], [sin, cos]])
    inverse = np.block([[cos, sin], [-sin, cos]])
    freqs = np.array([flipped(f) for f in range(OUTER)]) + SHIFT
    turn = 2.0 * math.pi * freqs[:, None] * at[None, :] / LENGTH

    def halves(matrix):
        high = matrix.astype(ml_dtypes.bfloat16)
        low = (matrix - high.astype(np.float64)).astype(ml_dtypes.bfloat16)
        return np.stack([high, low])

    twiddle = np.stack([np.cos(turn), np.sin(turn)]).astype(np.float32)
    return halves(forward), halves(inverse / LENGTH), twiddle


def times(pair, turn):
    re, im = pair
    turn = turn % 1.0
    if turn == 0.0:
        return pair
    if turn == 0.25:
        return (-im, re)
    if turn == 0.5:
        return (-re, -im)
    if turn == 0.75:
        return (im, -re)
    c, s = math.cos(2 * math.pi * turn), math.sin(2 * math.pi * turn)
    return (re * c - im * s, re * s + im * c)


def outer_forward(blocks):
    data = []
    for a, block in enumerate(blocks):
        angle = -2.0 * math.pi * a * SHIFT / OUTER
        data.append((block * math.cos(angle), block * math.sin(angle)) if a else (block, jnp.zeros_like(block)))
    half = OUTER // 2
    while half >= 1:
        for start in range(0, OUTER, 2 * half):
            for k in range(half):
                a, b = data[start + k], data[start + k + half]
                data[start + k] = (a[0] + b[0], a[1] + b[1])
                data[start + k + half] = times((a[0] - b[0], a[1] - b[1]), -k / (2 * half))
        half //= 2
    return data


def outer_inverse(data):
    data = list(data)
    half = 1
    while half < OUTER:
        for start in range(0, OUTER, 2 * half):
            for k in range(half):
                a, b = data[start + k], times(data[start + k + half], k / (2 * half))
                data[start + k] = (a[0] + b[0], a[1] + b[1])
                data[start + k + half] = (a[0] - b[0], a[1] - b[1])
        half *= 2
    out = []
    for a, (re, im) in enumerate(data):
        angle = 2.0 * math.pi * a * SHIFT / OUTER
        out.append(re * math.cos(angle) - im * math.sin(angle))
    return out


class Spread:
    def __init__(self, place, links, part, bufs):
        self.place, self.links, self.part = place, links, part
        self.z1, self.z2, self.zx, self.x1, self.x2, self.x3 = bufs
        self.pending = {}

    def cell(self, own, step, piece, half):
        return self.part(self.place.owner(own, step), piece, half)

    def send(self, key, src, dst, to):
        self.pending[key] = self.links.send(src, dst, to)

    def start_z1(self, own):
        for way in (0, 1):
            self.send(("z1", own, way), self.cell(own, 2, 0, way), self.z1.at[way, own], self.place.zway[way])

    def start_x1(self, step):
        for half in (0, 1):
            self.send(("x1", step, half), self.cell(0, step, 1, half), self.x1.at[step, half], self.place.far)

    def start_z2_free(self, own, way):
        step = (1, 3)[way]
        self.send(("z2", own, way, 1 - way), self.cell(own, step, 0, 1 - way), self.z2.at[way, own, 1 - way], self.place.zway[way])

    def pass_z1(self, own, way):
        self.pending[("z1", own, way)].wait_recv()
        cell = self.cell(own, (1, 3)[way], 0, way)
        cell[...] = (cell[...].astype(F32) + self.z1[way, own].astype(F32)).astype(BF)
        self.send(("z2", own, way, way), cell, self.z2.at[way, own, way], self.place.zway[way])

    def take_x1(self, step):
        for half in (0, 1):
            self.pending[("x1", step, half)].wait_recv()
            cell = self.cell(1, step, 1, half)
            cell[...] = (cell[...].astype(F32) + self.x1[step, half].astype(F32)).astype(BF)

    def start_x2(self):
        for way in (0, 1):
            self.send(("x2", way), self.cell(1, 2, 1, way), self.x2.at[way], self.place.zway[way])

    def start_x3_free(self, way):
        self.send(("x3", way, 1 - way), self.cell(1, (1, 3)[way], 1, 1 - way), self.x3.at[way, 1 - way], self.place.zway[way])

    def pass_x2(self, way):
        self.pending[("x2", way)].wait_recv()
        cell = self.cell(1, (1, 3)[way], 1, way)
        cell[...] = (cell[...].astype(F32) + self.x2[way].astype(F32)).astype(BF)
        self.send(("x3", way, way), cell, self.x3.at[way, way], self.place.zway[way])

    def wait_z2(self, own):
        for way in (0, 1):
            for half in (0, 1):
                self.pending[("z2", own, way, half)].wait_recv()

    def start_zx(self):
        self.wait_z2(0)
        for half in (0, 1):
            cell = self.cell(0, 0, 0, half)
            total = cell[...].astype(F32) + self.z2[0, 0, half].astype(F32) + self.z2[1, 0, half].astype(F32)
            cell[...] = total.astype(BF)
            self.send(("zx", half), cell, self.zx.at[half], self.place.far)

    def finish(self):
        self.wait_z2(1)
        for half in (0, 1):
            self.pending[("x1", 0, half)].wait_recv()
            for way in (0, 1):
                self.pending[("x3", way, half)].wait_recv()
        for half in (0, 1):
            self.pending[("zx", half)].wait_recv()

    def total(self, piece, half):
        mine = self.cell(1, 0, piece, half)[...].astype(F32)
        if piece == 0:
            terms = (self.z2[0, 1, half], self.z2[1, 1, half], self.zx[half])
        else:
            terms = (self.x1[0, half], self.x3[0, half], self.x3[1, half])
        for term in terms:
            mine = mine + term.astype(F32)
        return mine


class Place:
    def __init__(self, depth, tp_count, ctx_count):
        self.ctx, self.tp = lax.axis_index("ctx"), lax.axis_index("tp")
        self.depth, self.tp_count, self.ctx_count = depth, tp_count, ctx_count
        self.x_half, self.z = self.tp // depth, self.tp % depth
        self.zway = tuple((self.ctx, self.x_half * depth + (self.z + step) % depth) for step in (1, depth - 1))
        self.far = (self.ctx, (self.tp + depth) % tp_count)

    def owner(self, own, step):
        half = self.x_half if own else 1 - self.x_half
        return half * self.depth + (self.z + step) % self.depth


class Links:
    def __init__(self, send_sems, recv_sems):
        self.send_sems, self.recv_sems = send_sems, recv_sems
        self.used = 0
        self.started = []

    def make(self, src, dst, to, at):
        return pltpu.make_async_remote_copy(
            src_ref=src,
            dst_ref=dst,
            send_sem=self.send_sems.at[at],
            recv_sem=self.recv_sems.at[at],
            device_id=to,
            device_id_type=pl.DeviceIdType.MESH,
        )

    def send(self, src, dst, to):
        copy = self.make(src, dst, to, self.used)
        self.used += 1
        copy.start()
        self.started.append(copy)
        return copy


class Swap:
    def __init__(self, links, count, me, device, src, dst):
        self.links, self.count, self.me, self.device, self.src, self.dst = links, count, me, device, src, dst
        self.base = links.used
        links.used += count - 1

    def copy(self, away):
        peer = (self.me + away) % self.count
        return self.links.make(self.src(peer), self.dst(self.me), self.device(peer), self.base + away - 1)

    def each(self, act):
        lax.fori_loop(1, self.count, lambda away, carry: (act(self.copy(away)), carry)[1], 0)

    def start(self):
        self.each(lambda copy: copy.start())

    def wait_recv(self):
        self.each(lambda copy: copy.wait_recv())

    def wait_send(self):
        self.each(lambda copy: copy.wait_send())


def transposed(source, target, rows, lanes):
    for r in range(0, rows, 128):
        for c in range(0, lanes, 128):
            tile = source[pl.ds(r, 128), pl.ds(c, 128)].astype(F32)
            target[pl.ds(c, 128), pl.ds(r, 128)] = tile.T.astype(target.dtype)


def spectrum(source, staged, twiddle):
    ctx_count, lanes, span = source.shape
    fold = span // INNER

    def group(g, carry):
        at = pl.multiple_of(g * 16, 16)
        blocks = []
        for i in range(ctx_count):
            for u in range(fold):
                blocks.append(source[i, pl.ds(at, 16), pl.ds(u * INNER, INNER)].astype(F32))
        for f, (re, im) in enumerate(outer_forward(blocks)):
            c, s = twiddle[0, pl.ds(f, 1), :], twiddle[1, pl.ds(f, 1), :]
            row = pl.ds(pl.multiple_of(f * lanes + at, 16), 16)
            staged[row, pl.ds(0, INNER)] = (re * c + im * s).astype(BF)
            staged[row, pl.ds(INNER, INNER)] = (im * c - re * s).astype(BF)
        return carry

    lax.fori_loop(0, lanes // 16, group, 0)


def both(data, matrix):
    return jnp.dot(data, matrix[0], preferred_element_type=F32) + jnp.dot(data, matrix[1], preferred_element_type=F32)


def kernel(
    act, weight, taps, blocks, gains, forward, inverse, twiddle,
    out,
    wbuf, kv, qs,
    kv_z1, kv_z2, kv_zx, kv_x1, kv_x2, kv_x3,
    q_z1, q_z2, q_zx, q_x1, q_x2, q_x3,
    taps_in, taps_t, filt_in, staged, filt_spec,
    gated, gated_t, gated_in, mixed, conv_out, conv_in, conv_t, conv_home, conv_final,
    w_sems, send_sems, recv_sems,
    *, depth, tp_count, ctx_count,
):
    place = Place(depth, tp_count, ctx_count)
    me, tp = place.ctx, place.tp
    tokens, width = gated.shape
    lanes = width // ctx_count
    out_tokens = tokens // tp_count
    channels = tp_count * width
    tile = wbuf.shape[2]

    order = [(0, 2), (1, 2), (0, 1), (0, 3), (1, 1), (1, 3), (0, 0), (1, 0)]
    columns = []
    for own, step in order:
        for which in (1, 2):
            columns.append(which * channels + place.owner(own, step) * width)
    for t in range(channels // tile):
        columns.append(t * tile)

    def fetch(t):
        return pltpu.make_async_copy(weight.at[:, pl.ds(pl.multiple_of(columns[t], tile), tile)], wbuf.at[t], w_sems.at[t])

    ahead = 8
    for t in range(ahead):
        fetch(t).start()

    barrier = pltpu.get_barrier_semaphore()

    def greet(device, count, mine):
        def body(away, carry):
            pl.semaphore_signal(barrier, inc=1, device_id=device((mine + away) % count), device_id_type=pl.DeviceIdType.MESH)
            return carry
        lax.fori_loop(1, count, body, 0)

    greet(lambda peer: (me, peer), tp_count, tp)
    greet(lambda peer: (peer, tp), ctx_count, me)
    pl.semaphore_wait(barrier, tp_count + ctx_count - 2)

    links = Links(send_sems, recv_sems)

    def over_tp(src, dst):
        return Swap(links, tp_count, tp, lambda peer: (me, peer), src, dst)

    def over_ctx(src, dst):
        return Swap(links, ctx_count, me, lambda peer: (peer, tp), src, dst)

    def wide(ref, index, size):
        return ref.at[pl.ds(pl.multiple_of(index * size, size), size)]

    tap_swap = over_tp(lambda peer: taps.at[:, pl.ds(pl.multiple_of(peer * width, width), width)], lambda mine: wide(taps_in, mine, out_tokens))
    filt_swap = over_ctx(lambda peer: wide(taps_t, peer, lanes), lambda mine: filt_in.at[mine])
    gated_swap = over_ctx(lambda peer: wide(gated_t, peer, lanes), lambda mine: gated_in.at[mine])
    conv_swap = over_ctx(lambda peer: conv_out.at[peer], lambda mine: wide(conv_in, mine, lanes))
    home_swap = over_tp(lambda peer: wide(conv_home, peer, out_tokens), lambda mine: conv_final.at[mine])

    def kv_part(owner, piece, half):
        rows = pl.ds(0, ROWS_Z) if piece == 0 else pl.ds(ROWS_Z, tokens - ROWS_Z)
        return kv.at[owner, rows, pl.ds(half * width, width)]

    z_half, x_half = LANES_Z // 2, (channels - LANES_Z) // 2

    def q_part(owner, piece, half):
        return qs.at[owner, :, pl.ds(half * z_half, z_half) if piece == 0 else pl.ds(LANES_Z + half * x_half, x_half)]

    first = Spread(place, links, kv_part, (kv_z1, kv_z2, kv_zx, kv_x1, kv_x2, kv_x3))
    second = Spread(place, links, q_part, (q_z1, q_z2, q_zx, q_x1, q_x2, q_x3))

    tap_swap.start()

    sub = 256
    for n, (own, step) in enumerate(order):
        owner = place.owner(own, step)
        for which in (0, 1):
            t = 2 * n + which
            fetch(t).wait()
            if t + ahead < len(columns):
                fetch(t + ahead).start()

            def multiply(s, carry):
                at = pl.ds(pl.multiple_of(s * sub, sub), sub)
                to = pl.ds(pl.multiple_of(which * width + s * sub, sub), sub)
                kv[owner, :, to] = jnp.dot(act[...], wbuf[t, :, at], preferred_element_type=F32).astype(BF)
                return carry

            lax.fori_loop(0, width // sub, multiply, 0)
        if step == 2:
            first.start_z1(own)
        elif step == 1:
            first.start_z2_free(own, 0)
        elif step == 3:
            first.start_z2_free(own, 1)
        if own == 0:
            first.start_x1(step)

    tap_swap.wait_recv()
    wide(taps_in, tp, out_tokens)[...] = taps[:, pl.ds(pl.multiple_of(tp * width, width), width)]
    live = me < blocks[pl.ds(tp, 1), :]
    for r in range(0, tokens, 128):
        for c in range(0, width, 128):
            block = taps_in[pl.ds(r, 128), pl.ds(c, 128)].astype(F32)
            block = jnp.where(live[:, c:c + 128], block, 0.0)
            taps_t[pl.ds(c, 128), pl.ds(r, 128)] = block.T.astype(BF)
    filt_swap.start()

    for own in (0, 1):
        for way in (0, 1):
            first.pass_z1(own, way)

    for t in range(2 * len(order), len(columns)):
        fetch(t).wait()
        if t + ahead < len(columns):
            fetch(t + ahead).start()

        def multiply(s, carry):
            at = pl.ds(pl.multiple_of(s * sub, sub), sub)
            to = pl.ds(pl.multiple_of((t - 2 * len(order)) * tile + s * sub, sub), sub)
            block = jnp.dot(act[...], wbuf[t, :, at], preferred_element_type=F32).astype(BF)
            qs[:, :, to] = block.reshape(tp_count, out_tokens, sub)
            return carry

        lax.fori_loop(0, tile // sub, multiply, 0)

    first.take_x1(2)
    first.start_x2()
    first.take_x1(1)
    first.start_x3_free(0)
    first.take_x1(3)
    first.start_x3_free(1)

    filt_swap.wait_recv()
    filt_in[me] = wide(taps_t, me, lanes)[...]
    spectrum(filt_in, staged, twiddle)
    rows = staged.shape[0] // 4

    def filter_tile(n, carry):
        at = pl.ds(pl.multiple_of(n * rows, rows), rows)
        filt_spec[at, :] = both(staged[at, :], forward)
        return carry

    lax.fori_loop(0, 4, filter_tile, 0)

    first.start_zx()
    for way in (0, 1):
        first.pass_x2(way)

    for own in (0, 1):
        second.start_z1(own)
    for step in (2, 1, 3, 0):
        second.start_x1(step)
    for own in (0, 1):
        for way in (0, 1):
            second.start_z2_free(own, way)

    first.finish()
    for piece, at in ((0, pl.ds(0, ROWS_Z)), (1, pl.ds(ROWS_Z, tokens - ROWS_Z))):
        gated[at, :] = first.total(piece, 0) * first.total(piece, 1)
    transposed(gated, gated_t, tokens, width)
    gated_swap.start()

    for own in (0, 1):
        for way in (0, 1):
            second.pass_z1(own, way)
    second.take_x1(2)
    second.start_x2()
    second.take_x1(1)
    second.start_x3_free(0)
    second.take_x1(3)
    second.start_x3_free(1)

    gated_swap.wait_recv()
    gated_in[me] = wide(gated_t, me, lanes)[...]
    spectrum(gated_in, staged, twiddle)
    per = rows // lanes

    def mix_tile(n, carry):
        at = pl.ds(pl.multiple_of(n * rows, rows), rows)
        a = both(staged[at, :], forward)
        b = filt_spec[at, :]
        a_re, a_im, b_re, b_im = a[:, :INNER], a[:, INNER:], b[:, :INNER], b[:, INNER:]
        prod = jnp.concatenate([a_re * b_re - a_im * b_im, a_re * b_im + a_im * b_re], axis=1)
        mixed[at, :] = both(prod.astype(BF), inverse)
        return carry

    lax.fori_loop(0, 4, mix_tile, 0)

    def unmix(g, carry):
        at = pl.multiple_of(g * 16, 16)
        data = []
        for f in range(OUTER):
            c, s = twiddle[0, pl.ds(f, 1), :], twiddle[1, pl.ds(f, 1), :]
            row = pl.ds(pl.multiple_of(f * lanes + at, 16), 16)
            re, im = mixed[row, pl.ds(0, INNER)], mixed[row, pl.ds(INNER, INNER)]
            data.append((re * c - im * s, re * s + im * c))
        fold = tokens // INNER
        for a, block in enumerate(outer_inverse(data)):
            conv_out[a // fold, pl.ds(at, 16), pl.ds(a % fold * INNER, INNER)] = block.astype(BF)
        return carry

    lax.fori_loop(0, lanes // 16, unmix, 0)
    conv_swap.start()

    second.start_zx()
    for way in (0, 1):
        second.pass_x2(way)

    conv_swap.wait_recv()
    wide(conv_in, me, lanes)[...] = conv_out[me]
    transposed(conv_in, conv_t, width, tokens)
    conv_home[...] = (conv_t[...] + gains[pl.ds(tp, 1), :] * gated[...]).astype(BF)
    home_swap.start()

    second.finish()
    home_swap.wait_recv()
    conv_final[tp] = wide(conv_home, tp, out_tokens)[...]
    query = jnp.concatenate([second.total(piece, half) for piece in (0, 1) for half in (0, 1)], axis=1)
    for j in range(tp_count):
        at = slice(j * width, (j + 1) * width)
        out[:, at] = (query[:, at] * conv_final[j].astype(F32)).astype(BF)

    for copy in links.started:
        copy.wait_send()
    for swap in (tap_swap, filt_swap, gated_swap, conv_swap, home_swap):
        swap.wait_send()


def on_device(activations, proj_weight, filter_taps, filter_blocks, skip_gain):
    tokens, depth_here = activations.shape
    channels, out_tokens = filter_taps.shape
    tp_count, ctx_count = lax.axis_size("tp"), lax.axis_size("ctx")
    depth = 4
    width = channels // tp_count
    lanes = width // ctx_count
    forward, inverse, twiddle = tables()

    def buffers(z_rows, z_lanes, x_rows, x_lanes):
        return [
            pltpu.VMEM((2, 2, z_rows, z_lanes), BF),
            pltpu.VMEM((2, 2, 2, z_rows, z_lanes), BF),
            pltpu.VMEM((2, z_rows, z_lanes), BF),
            pltpu.VMEM((4, 2, x_rows, x_lanes), BF),
            pltpu.VMEM((2, x_rows, x_lanes), BF),
            pltpu.VMEM((2, 2, x_rows, x_lanes), BF),
        ]

    tile = 512
    n_copies = 2 * 28 + 2 * (tp_count - 1) + 3 * (ctx_count - 1)
    spec_rows = OUTER * lanes
    scratch = (
        [
            pltpu.VMEM((3 * channels // tile, depth_here, tile), BF),
            pltpu.VMEM((tp_count, tokens, 2 * width), BF),
            pltpu.VMEM((tp_count, out_tokens, channels), BF),
        ]
        + buffers(ROWS_Z, width, tokens - ROWS_Z, width)
        + buffers(out_tokens, LANES_Z // 2, out_tokens, (channels - LANES_Z) // 2)
        + [
            pltpu.VMEM((tokens, width), BF),
            pltpu.VMEM((width, tokens), BF),
            pltpu.VMEM((ctx_count, lanes, tokens), BF),
            pltpu.VMEM((spec_rows, 2 * INNER), BF),
            pltpu.VMEM((spec_rows, 2 * INNER), F32),
            pltpu.VMEM((tokens, width), F32),
            pltpu.VMEM((width, tokens), BF),
            pltpu.VMEM((ctx_count, lanes, tokens), BF),
            pltpu.VMEM((spec_rows, 2 * INNER), F32),
            pltpu.VMEM((ctx_count, lanes, tokens), BF),
            pltpu.VMEM((width, tokens), BF),
            pltpu.VMEM((tokens, width), F32),
            pltpu.VMEM((tokens, width), BF),
            pltpu.VMEM((tp_count, out_tokens, width), BF),
            pltpu.SemaphoreType.DMA((3 * channels // tile,)),
            pltpu.SemaphoreType.DMA((n_copies,)),
            pltpu.SemaphoreType.DMA((n_copies,)),
        ]
    )
    vmem = pl.BlockSpec(memory_space=pltpu.VMEM)
    out = pl.pallas_call(
        functools.partial(kernel, depth=depth, tp_count=tp_count, ctx_count=ctx_count),
        out_shape=jax.ShapeDtypeStruct((out_tokens, channels), BF),
        in_specs=[vmem, pl.BlockSpec(memory_space=pl.ANY)] + [vmem] * 6,
        out_specs=vmem,
        scratch_shapes=scratch,
        compiler_params=pltpu.CompilerParams(collective_id=0, has_side_effects=True, vmem_limit_bytes=60 * 2**20),
        name="hyena",
    )(
        activations,
        proj_weight,
        filter_taps.T.astype(BF),
        filter_blocks.reshape(tp_count, width),
        skip_gain.reshape(tp_count, width),
        jnp.asarray(forward),
        jnp.asarray(inverse),
        jnp.asarray(twiddle),
    )
    return out.T


def solution(mesh):
    placed = (P("ctx", "tp"), P("tp", None), P(None, ("ctx", "tp")), P(), P())
    return jax.shard_map(
        on_device, mesh=mesh, in_specs=placed, out_specs=P(None, ("ctx", "tp")), check_vma=False
    )
```

profile of v0, /device:TPU:1, one launch (start us, length us, event | category | flops | bytes accessed | tf_op | source)
XLA Modules:
  0.0 83.1 jit_solution(7064178994578514704)
XLA Ops:
  0.0 1.3 %reshape.6.blocks = s32[8,512]{1,0:T(8,128)} reshape(s32[4096]{0:T(1024)} %param.11) | data formatting | bytes 32768 | tf_op jit(solution)/shard_map/reshape | solution.py:563
  1.3 1.3 %reshape.7.gains = f32[8,512]{1,0:T(8,128)} reshape(f32[4096]{0:T(1024)} %param.12) | data formatting | bytes 32768 | tf_op jit(solution)/shard_map/reshape | solution.py:564
  2.6 1.8 %convert_bitcast_fusion.taps = bf16[32,4096]{1,0:T(8,128)(2,1)} fusion(f32[4096,32]{0,1:T(8,128)} %param.10), kind=kLoop, calls=%fused_computation | loop fusion | flops 131072 | bytes 786432 | tf_op jit(solution)/shard_map/convert_element_type | solution.py:562
  4.4 77.0 %hyena.1 = bf16[32,4096]{1,0:T(8,128)(2,1)} custom-call(bf16[256,1024]{1,0:T(8,128)(2,1)} %act.1, bf16[1024,12288]{1,0:T(8,128)(2,1)} %weight.1, bf16[32,4096]{1,0:T(8,128)(2,1)} %convert_bitcast_fusion.taps, s32[8,512]{1,0:T(8,128)} %reshape.6.blocks, f32[8,512]{1,0:T(8,128)} %reshape.7.gains, bf16[2,256,256]{2,1,0:T(8,128)(2,1)} %constant.6.clone.forward, ...), custom_call_target="tpu_custom_call" | custom-call | tf_op jit(solution)/shard_map/hyena/pallas_call | solution.py:551
  81.4 1.7 %copy.10 = bf16[4096,32]{0,1:T(8,128)(2,1)} copy(bf16[4096,32]{0,1:T(8,128)(2,1)} %bitcast.3) | data formatting | bytes 524288
where the time goes:
time: 83.4 us; the launch traced here: 83.1 us
  Pallas kernels  77 us (92%)
  local copies, waits for them, and re-layouts  4.3 us (5%)
  other arithmetic  1.77 us (2%)
    pallas_call x1, Pallas kernels, on_device(): pl.pallas_call(functools.partial(kernel, depth=depth, tp_count=tp_count,...  77 us
    convert_element_type x1, other arithmetic, on_device(): filter_taps.T.astype(BF)  1.77 us
    unnamed x1, local copies, waits for them, and re-layouts  1.67 us

commit v1 on v0

v1 whole, which is shorter than its diff:
```python
import functools
import math

import jax
import jax.numpy as jnp
import ml_dtypes
import numpy as np
from jax import lax
from jax.experimental import pallas as pl
from jax.experimental.pallas import tpu as pltpu
from jax.sharding import PartitionSpec as P

BF = jnp.bfloat16
F32 = jnp.float32
OUTER = 32
INNER = 128
LENGTH = OUTER * INNER
SETS = 2
SHIFT = 0.25

ROWS_Z = 160
LANES_Z = 2816

SCHEDULE = (
    ("mm", 0, 2), ("mm", 1, 2), ("bar",), ("x1", 0, 2), ("z1", 0, 0), ("tap",), ("z1", 0, 1), ("x1", 1, 2), ("mm", 0, 1),
    ("mm", 0, 3), ("x1", 0, 1), ("z2f", 0, 0, 1), ("mm", 1, 1), ("mm", 1, 3), ("pz1", 0, 0, 0), ("z2f", 0, 1, 1), ("x1", 0, 3),
    ("tx1", 0, 2), ("mm", 0, 0), ("x1", 0, 0), ("x2", 0), ("z2f", 1, 0, 0), ("z2f", 0, 0, 0), ("pz1", 0, 0, 1), ("z1", 1, 0),
    ("x1", 1, 1), ("mm", 1, 0), ("tx1", 1, 2), ("mq", 0), ("mq", 1), ("pz1", 0, 1, 1), ("pz1", 0, 1, 0), ("zx", 0, 0), ("x2", 1),
    ("z2f", 0, 1, 0), ("mask",), ("zx", 0, 1), ("tx1", 0, 3), ("x3f", 0, 1), ("px2", 0, 1), ("tx1", 0, 1), ("x3f", 0, 0),
    ("px2", 0, 0), ("z2f", 1, 0, 1), ("mq", 2), ("pz1", 1, 0, 0), ("pz1", 1, 0, 1), ("x1", 1, 3), ("tx1", 1, 1), ("z1", 1, 1),
    ("x1", 1, 0), ("mq", 3), ("px2", 1, 0), ("z2f", 1, 1, 1), ("x1", 2, 2), ("z2f", 2, 0, 0), ("filt",), ("fin", 0), ("gate", 0),
    ("zx", 1, 1), ("zx", 1, 0), ("pz1", 1, 1, 0), ("pz1", 1, 1, 1), ("tx1", 1, 3), ("x3f", 1, 1), ("x1", 2, 1), ("px2", 1, 1),
    ("z2f", 1, 1, 0), ("x3f", 1, 0), ("z1", 2, 0), ("z2f", 2, 0, 1), ("x1", 2, 3), ("tx1", 2, 2), ("z2f", 2, 1, 0), ("conv", 0),
    ("fin", 1), ("gate", 1), ("pz1", 2, 0, 1), ("pz1", 2, 0, 0), ("tx1", 2, 1), ("x3f", 2, 0), ("x2", 2), ("tx1", 2, 3),
    ("x3f", 2, 1), ("x1", 2, 0), ("z2f", 2, 1, 1), ("z1", 2, 1), ("home", 0), ("conv", 1), ("px2", 2, 0), ("px2", 2, 1),
    ("zx", 2, 1), ("zx", 2, 0), ("pz1", 2, 1, 0), ("pz1", 2, 1, 1), ("home", 1), ("fin", 2), ("out",),
)


def flipped(index):
    return int(format(index, "05b")[::-1], 2)


def tables():
    at = np.arange(INNER)
    angle = 2.0 * math.pi * (at[:, None] * at[None, :] % INNER) / INNER
    cos, sin = np.cos(angle), np.sin(angle)
    forward = np.block([[cos, -sin], [sin, cos]])
    inverse = np.block([[cos, sin], [-sin, cos]])
    freqs = np.array([flipped(f) for f in range(OUTER)]) + SHIFT
    turn = 2.0 * math.pi * freqs[:, None] * at[None, :] / LENGTH

    def halves(matrix):
        high = matrix.astype(ml_dtypes.bfloat16)
        low = (matrix - high.astype(np.float64)).astype(ml_dtypes.bfloat16)
        return np.stack([high, low])

    twiddle = np.stack([np.cos(turn), np.sin(turn)]).astype(np.float32)
    return halves(forward), halves(inverse / LENGTH), twiddle


def times(pair, turn):
    re, im = pair
    turn = turn % 1.0
    if turn == 0.0:
        return pair
    if turn == 0.25:
        return (-im, re)
    if turn == 0.5:
        return (-re, -im)
    if turn == 0.75:
        return (im, -re)
    c, s = math.cos(2 * math.pi * turn), math.sin(2 * math.pi * turn)
    return (re * c - im * s, re * s + im * c)


def outer_forward(blocks):
    data = []
    for a, block in enumerate(blocks):
        angle = -2.0 * math.pi * a * SHIFT / OUTER
        data.append((block * math.cos(angle), block * math.sin(angle)) if a else (block, jnp.zeros_like(block)))
    half = OUTER // 2
    while half >= 1:
        for start in range(0, OUTER, 2 * half):
            for k in range(half):
                a, b = data[start + k], data[start + k + half]
                data[start + k] = (a[0] + b[0], a[1] + b[1])
                data[start + k + half] = times((a[0] - b[0], a[1] - b[1]), -k / (2 * half))
        half //= 2
    return data


def outer_inverse(data):
    data = list(data)
    half = 1
    while half < OUTER:
        for start in range(0, OUTER, 2 * half):
            for k in range(half):
                a, b = data[start + k], times(data[start + k + half], k / (2 * half))
                data[start + k] = (a[0] + b[0], a[1] + b[1])
                data[start + k + half] = (a[0] - b[0], a[1] - b[1])
        half *= 2
    out = []
    for a, (re, im) in enumerate(data):
        angle = 2.0 * math.pi * a * SHIFT / OUTER
        out.append(re * math.cos(angle) - im * math.sin(angle))
    return out


class Spread:
    def __init__(self, place, links, part, bufs):
        self.place, self.links, self.part = place, links, part
        self.z1, self.z2, self.zx, self.x1, self.x2, self.x3 = bufs
        self.pending = {}

    def cell(self, own, step, piece, half):
        return self.part(self.place.owner(own, step), piece, half)

    def send(self, key, src, dst, to):
        self.pending[key] = self.links.send(src, dst, to)

    def start_z1(self, own):
        for way in (0, 1):
            self.send(("z1", own, way), self.cell(own, 2, 0, way), self.z1.at[way, own], self.place.zway[way])

    def start_x1(self, step):
        for half in (0, 1):
            self.send(("x1", step, half), self.cell(0, step, 1, half), self.x1.at[step, half], self.place.far)

    def start_z2_free(self, own, way):
        step = (1, 3)[way]
        self.send(("z2", own, way, 1 - way), self.cell(own, step, 0, 1 - way), self.z2.at[way, own, 1 - way], self.place.zway[way])

    def pass_z1(self, own, way):
        self.pending[("z1", own, way)].wait_recv()
        cell = self.cell(own, (1, 3)[way], 0, way)
        cell[...] = (cell[...].astype(F32) + self.z1[way, own].astype(F32)).astype(BF)
        self.send(("z2", own, way, way), cell, self.z2.at[way, own, way], self.place.zway[way])

    def take_x1(self, step):
        for half in (0, 1):
            self.pending[("x1", step, half)].wait_recv()
            cell = self.cell(1, step, 1, half)
            cell[...] = (cell[...].astype(F32) + self.x1[step, half].astype(F32)).astype(BF)

    def start_x2(self):
        for way in (0, 1):
            self.send(("x2", way), self.cell(1, 2, 1, way), self.x2.at[way], self.place.zway[way])

    def start_x3_free(self, way):
        self.send(("x3", way, 1 - way), self.cell(1, (1, 3)[way], 1, 1 - way), self.x3.at[way, 1 - way], self.place.zway[way])

    def pass_x2(self, way):
        self.pending[("x2", way)].wait_recv()
        cell = self.cell(1, (1, 3)[way], 1, way)
        cell[...] = (cell[...].astype(F32) + self.x2[way].astype(F32)).astype(BF)
        self.send(("x3", way, way), cell, self.x3.at[way, way], self.place.zway[way])

    def start_zx(self, half):
        for way in (0, 1):
            self.pending[("z2", 0, way, half)].wait_recv()
        cell = self.cell(0, 0, 0, half)
        total = cell[...].astype(F32) + self.z2[0, 0, half].astype(F32) + self.z2[1, 0, half].astype(F32)
        cell[...] = total.astype(BF)
        self.send(("zx", half), cell, self.zx.at[half], self.place.far)

    def finish(self):
        for half in (0, 1):
            self.pending[("x1", 0, half)].wait_recv()
            for way in (0, 1):
                self.pending[("z2", 1, way, half)].wait_recv()
                self.pending[("x3", way, half)].wait_recv()
            self.pending[("zx", half)].wait_recv()

    def total(self, piece, half):
        mine = self.cell(1, 0, piece, half)[...].astype(F32)
        if piece == 0:
            terms = (self.z2[0, 1, half], self.z2[1, 1, half], self.zx[half])
        else:
            terms = (self.x1[0, half], self.x3[0, half], self.x3[1, half])
        for term in terms:
            mine = mine + term.astype(F32)
        return mine


class Place:
    def __init__(self, depth, tp_count, ctx_count):
        self.ctx, self.tp = lax.axis_index("ctx"), lax.axis_index("tp")
        self.depth, self.tp_count, self.ctx_count = depth, tp_count, ctx_count
        self.x_half, self.z = self.tp // depth, self.tp % depth
        self.zway = tuple((self.ctx, self.x_half * depth + (self.z + step) % depth) for step in (1, depth - 1))
        self.far = (self.ctx, (self.tp + depth) % tp_count)

    def owner(self, own, step):
        half = self.x_half if own else 1 - self.x_half
        return half * self.depth + (self.z + step) % self.depth


class Links:
    def __init__(self, send_sems, recv_sems):
        self.send_sems, self.recv_sems = send_sems, recv_sems
        self.used = 0
        self.started = []

    def make(self, src, dst, to, at):
        return pltpu.make_async_remote_copy(
            src_ref=src,
            dst_ref=dst,
            send_sem=self.send_sems.at[at],
            recv_sem=self.recv_sems.at[at],
            device_id=to,
            device_id_type=pl.DeviceIdType.MESH,
        )

    def send(self, src, dst, to):
        copy = self.make(src, dst, to, self.used)
        self.used += 1
        copy.start()
        self.started.append(copy)
        return copy


class Swap:
    def __init__(self, links, count, me, device, src, dst):
        self.links, self.count, self.me, self.device, self.src, self.dst = links, count, me, device, src, dst
        self.base = links.used
        links.used += count - 1

    def copy(self, away):
        peer = (self.me + away) % self.count
        return self.links.make(self.src(peer), self.dst(self.me), self.device(peer), self.base + away - 1)

    def each(self, act):
        lax.fori_loop(1, self.count, lambda away, carry: (act(self.copy(away)), carry)[1], 0)

    def start(self):
        self.each(lambda copy: copy.start())

    def wait_recv(self):
        self.each(lambda copy: copy.wait_recv())

    def wait_send(self):
        self.each(lambda copy: copy.wait_send())


def transposed(source, target, rows, lanes):
    for r in range(0, rows, 128):
        for c in range(0, lanes, 128):
            tile = source[pl.ds(r, 128), pl.ds(c, 128)].astype(F32)
            target[pl.ds(c, 128), pl.ds(r, 128)] = tile.T.astype(target.dtype)


def spectrum(source, staged, twiddle):
    ctx_count, lanes, span = source.shape
    blocks = []
    for i in range(ctx_count):
        for u in range(span // INNER):
            blocks.append(source[i, :, pl.ds(u * INNER, INNER)].astype(F32))
    for f, (re, im) in enumerate(outer_forward(blocks)):
        c, s = twiddle[0, pl.ds(f, 1), :], twiddle[1, pl.ds(f, 1), :]
        staged[pl.ds(f * lanes, lanes), pl.ds(0, INNER)] = (re * c + im * s).astype(BF)
        staged[pl.ds(f * lanes, lanes), pl.ds(INNER, INNER)] = (im * c - re * s).astype(BF)


def both(data, matrix):
    return jnp.dot(data, matrix[0], preferred_element_type=F32) + jnp.dot(data, matrix[1], preferred_element_type=F32)


def kernel(
    act, weight, taps, blocks, gains, forward, inverse, twiddle,
    out,
    wbuf, kv, qs,
    a_z1, a_z2, a_zx, a_x1, a_x2, a_x3,
    b_z1, b_z2, b_zx, b_x1, b_x2, b_x3,
    q_z1, q_z2, q_zx, q_x1, q_x2, q_x3,
    taps_out, taps_in, taps_t, filt_in, staged, filt_spec,
    gated, gated_t, gated_in, mixed, conv_out, conv_in, conv_home, conv_final,
    w_sems, send_sems, recv_sems,
    *, depth, tp_count, ctx_count,
):
    place = Place(depth, tp_count, ctx_count)
    me, tp = place.ctx, place.tp
    tokens, width = gated.shape
    out_tokens = tokens // tp_count
    channels = tp_count * width
    tile = wbuf.shape[2]
    piece = width // SETS
    lanes = piece // ctx_count

    order = [step[1:] for step in SCHEDULE if step[0] == "mm"]
    tiles = []
    for own, step in order:
        base = place.owner(own, step) * width
        tiles.append([(which * channels + base + c * piece, piece) for c in range(SETS) for which in (1, 2)])
    for t in range(channels // tile):
        tiles.append([(t * tile, tile)])

    def fetch(t, act_on):
        at = 0
        for k, (column, size) in enumerate(tiles[t]):
            src = weight.at[:, pl.ds(pl.multiple_of(column, size), size)]
            act_on(pltpu.make_async_copy(src, wbuf.at[t, :, pl.ds(at, size)], w_sems.at[4 * t + k]))
            at += size

    ahead = 4
    for t in range(ahead):
        fetch(t, lambda copy: copy.start())

    def next_tile(t):
        fetch(t, lambda copy: copy.wait())
        if t + ahead < len(tiles):
            fetch(t + ahead, lambda copy: copy.start())

    barrier = pltpu.get_barrier_semaphore()

    def greet(device, count, mine):
        def body(away, carry):
            pl.semaphore_signal(barrier, inc=1, device_id=device((mine + away) % count), device_id_type=pl.DeviceIdType.MESH)
            return carry
        lax.fori_loop(1, count, body, 0)

    greet(lambda peer: (me, peer), tp_count, tp)
    greet(lambda peer: (peer, tp), ctx_count, me)

    taps_out[...] = taps[...].astype(BF)

    links = Links(send_sems, recv_sems)

    def over_tp(src, dst):
        return Swap(links, tp_count, tp, lambda peer: (me, peer), src, dst)

    def over_ctx(src, dst):
        return Swap(links, ctx_count, me, lambda peer: (peer, tp), src, dst)

    def span(index, size):
        return pl.ds(pl.multiple_of(index * size, size), size)

    tap_swap = over_tp(lambda peer: taps_out.at[:, span(peer, width)], lambda mine: taps_in.at[span(mine, out_tokens)])
    filt_swap = over_ctx(lambda peer: taps_t.at[:, span(peer, lanes)], lambda mine: filt_in.at[mine])
    gated_swap = [over_ctx(lambda peer, c=c: gated_t.at[c, span(peer, lanes)], lambda mine, c=c: gated_in.at[c, mine]) for c in range(SETS)]
    conv_swap = [over_ctx(lambda peer, c=c: conv_out.at[c, peer], lambda mine, c=c: conv_in.at[c, span(mine, lanes)]) for c in range(SETS)]
    home_swap = [over_tp(lambda peer, c=c: conv_home.at[c, span(peer, out_tokens)], lambda mine, c=c: conv_final.at[c, mine]) for c in range(SETS)]

    def kv_part(c):
        def part(owner, which, half):
            rows = pl.ds(0, ROWS_Z) if which == 0 else pl.ds(ROWS_Z, tokens - ROWS_Z)
            return kv.at[owner, rows, pl.ds((2 * c + half) * piece, piece)]
        return part

    z_half, x_half = LANES_Z // 2, (channels - LANES_Z) // 2

    def q_part(owner, which, half):
        return qs.at[owner, :, pl.ds(half * z_half, z_half) if which == 0 else pl.ds(LANES_Z + half * x_half, x_half)]

    spreads = (
        Spread(place, links, kv_part(0), (a_z1, a_z2, a_zx, a_x1, a_x2, a_x3)),
        Spread(place, links, kv_part(1), (b_z1, b_z2, b_zx, b_x1, b_x2, b_x3)),
        Spread(place, links, q_part, (q_z1, q_z2, q_zx, q_x1, q_x2, q_x3)),
    )

    def multiply_kv(own, step):
        t = order.index((own, step))
        next_tile(t)
        kv[place.owner(own, step)] = jnp.dot(act[...], wbuf[t], preferred_element_type=F32).astype(BF)

    def multiply_q(t):
        next_tile(len(order) + t)
        block = jnp.dot(act[...], wbuf[len(order) + t], preferred_element_type=F32).astype(BF)
        qs[:, :, pl.ds(t * tile, tile)] = block.reshape(tp_count, out_tokens, tile)

    def mask():
        tap_swap.wait_recv()
        taps_in[span(tp, out_tokens), :] = taps_out[:, span(tp, width)]
        live = me < blocks[span(tp, width)].reshape(1, width)
        for c in range(SETS):
            for r in range(0, tokens, 128):
                for k in range(0, piece, 128):
                    at = c * piece + k
                    block = taps_in[pl.ds(r, 128), pl.ds(at, 128)].astype(F32)
                    block = jnp.where(live[:, at:at + 128], block, 0.0)
                    taps_t[c, pl.ds(k, 128), pl.ds(r, 128)] = block.T.astype(BF)
        filt_swap.start()

    rows = staged.shape[1] // 2

    def filter_spectrum():
        filt_swap.wait_recv()
        filt_in[me] = taps_t[:, span(me, lanes), :]
        for c in range(SETS):
            spectrum(filt_in.at[:, c], staged.at[c], twiddle)
            for n in range(2):
                at = pl.ds(n * rows, rows)
                filt_spec[c, at, :] = both(staged[c, at, :], forward)

    def finish(c):
        spreads[c].finish()
        if c < SETS:
            for which, at in ((0, pl.ds(0, ROWS_Z)), (1, pl.ds(ROWS_Z, tokens - ROWS_Z))):
                gated[at, pl.ds(c * piece, piece)] = spreads[c].total(which, 0) * spreads[c].total(which, 1)

    def gate(c):
        transposed(gated.at[:, pl.ds(c * piece, piece)], gated_t.at[c], tokens, piece)
        gated_swap[c].start()

    def convolve(c):
        gated_swap[c].wait_recv()
        gated_in[c, me] = gated_t[c, span(me, lanes), :]
        spectrum(gated_in.at[c], staged.at[c], twiddle)
        for n in range(2):
            at = pl.ds(n * rows, rows)
            a, b = both(staged[c, at, :], forward), filt_spec[c, at, :]
            a_re, a_im, b_re, b_im = a[:, :INNER], a[:, INNER:], b[:, :INNER], b[:, INNER:]
            prod = jnp.concatenate([a_re * b_re - a_im * b_im, a_re * b_im + a_im * b_re], axis=1)
            mixed[at, :] = both(prod.astype(BF), inverse)
        data = []
        for f in range(OUTER):
            cos, sin = twiddle[0, pl.ds(f, 1), :], twiddle[1, pl.ds(f, 1), :]
            row = pl.ds(f * lanes, lanes)
            re, im = mixed[row, pl.ds(0, INNER)], mixed[row, pl.ds(INNER, INNER)]
            data.append((re * cos - im * sin, re * sin + im * cos))
        fold = tokens // INNER
        for a, block in enumerate(outer_inverse(data)):
            conv_out[c, a // fold, :, pl.ds(a % fold * INNER, INNER)] = block.astype(BF)
        conv_swap[c].start()

    def home(c):
        conv_swap[c].wait_recv()
        conv_in[c, span(me, lanes), :] = conv_out[c, me]
        gain = gains[span(tp, width)].reshape(1, width)
        for r in range(0, tokens, 128):
            for k in range(0, piece, 128):
                at = c * piece + k
                conv = conv_in[c, pl.ds(k, 128), pl.ds(r, 128)].astype(F32).T
                total = conv + gain[:, at:at + 128] * gated[pl.ds(r, 128), pl.ds(at, 128)]
                conv_home[c, pl.ds(r, 128), pl.ds(k, 128)] = total.astype(BF)
        home_swap[c].start()

    def finale():
        for c in range(SETS):
            home_swap[c].wait_recv()
            conv_final[c, tp] = conv_home[c, span(tp, out_tokens), :]
        query = jnp.concatenate([spreads[SETS].total(which, half) for which in (0, 1) for half in (0, 1)], axis=1)
        for j in range(tp_count):
            for c in range(SETS):
                at = slice(j * width + c * piece, j * width + (c + 1) * piece)
                out[:, at] = (query[:, at] * conv_final[c, j].astype(F32)).astype(BF)

    steps = {
        "bar": lambda: pl.semaphore_wait(barrier, tp_count + ctx_count - 2),
        "mm": multiply_kv,
        "mq": multiply_q,
        "tap": tap_swap.start,
        "mask": mask,
        "filt": filter_spectrum,
        "z1": lambda c, own: spreads[c].start_z1(own),
        "x1": lambda c, step: spreads[c].start_x1(step),
        "z2f": lambda c, own, way: spreads[c].start_z2_free(own, way),
        "pz1": lambda c, own, way: spreads[c].pass_z1(own, way),
        "tx1": lambda c, step: spreads[c].take_x1(step),
        "x2": lambda c: spreads[c].start_x2(),
        "x3f": lambda c, way: spreads[c].start_x3_free(way),
        "px2": lambda c, way: spreads[c].pass_x2(way),
        "zx": lambda c, half: spreads[c].start_zx(half),
        "fin": finish,
        "gate": gate,
        "conv": convolve,
        "home": home,
        "out": finale,
    }
    for step in SCHEDULE:
        steps[step[0]](*step[1:])

    for copy in links.started:
        copy.wait_send()
    for swap in [tap_swap, filt_swap] + gated_swap + conv_swap + home_swap:
        swap.wait_send()


def on_device(activations, proj_weight, filter_taps, filter_blocks, skip_gain):
    tokens, depth_here = activations.shape
    channels, out_tokens = filter_taps.shape
    tp_count, ctx_count = lax.axis_size("tp"), lax.axis_size("ctx")
    depth = 4
    width = channels // tp_count
    forward, inverse, twiddle = tables()

    def buffers(z_rows, z_lanes, x_rows, x_lanes):
        return [
            pltpu.VMEM((2, 2, z_rows, z_lanes), BF),
            pltpu.VMEM((2, 2, 2, z_rows, z_lanes), BF),
            pltpu.VMEM((2, z_rows, z_lanes), BF),
            pltpu.VMEM((4, 2, x_rows, x_lanes), BF),
            pltpu.VMEM((2, x_rows, x_lanes), BF),
            pltpu.VMEM((2, 2, x_rows, x_lanes), BF),
        ]

    tile = 2 * width
    n_tiles = 3 * channels // tile
    n_copies = (SETS + 1) * 28 + (1 + SETS) * (tp_count - 1) + (1 + 2 * SETS) * (ctx_count - 1)
    piece = width // SETS
    lanes = piece // ctx_count
    spec_rows = OUTER * lanes
    scratch = (
        [
            pltpu.VMEM((n_tiles, depth_here, tile), BF),
            pltpu.VMEM((tp_count, tokens, 2 * width), BF),
            pltpu.VMEM((tp_count, out_tokens, channels), BF),
        ]
        + buffers(ROWS_Z, piece, tokens - ROWS_Z, piece)
        + buffers(ROWS_Z, piece, tokens - ROWS_Z, piece)
        + buffers(out_tokens, LANES_Z // 2, out_tokens, (channels - LANES_Z) // 2)
        + [
            pltpu.VMEM((out_tokens, channels), BF),
            pltpu.VMEM((tokens, width), BF),
            pltpu.VMEM((SETS, piece, tokens), BF),
            pltpu.VMEM((ctx_count, SETS, lanes, tokens), BF),
            pltpu.VMEM((SETS, spec_rows, 2 * INNER), BF),
            pltpu.VMEM((SETS, spec_rows, 2 * INNER), F32),
            pltpu.VMEM((tokens, width), F32),
            pltpu.VMEM((SETS, piece, tokens), BF),
            pltpu.VMEM((SETS, ctx_count, lanes, tokens), BF),
            pltpu.VMEM((spec_rows, 2 * INNER), F32),
            pltpu.VMEM((SETS, ctx_count, lanes, tokens), BF),
            pltpu.VMEM((SETS, piece, tokens), BF),
            pltpu.VMEM((SETS, tokens, piece), BF),
            pltpu.VMEM((SETS, tp_count, out_tokens, piece), BF),
            pltpu.SemaphoreType.DMA((4 * n_tiles,)),
            pltpu.SemaphoreType.DMA((n_copies,)),
            pltpu.SemaphoreType.DMA((n_copies,)),
        ]
    )
    vmem = pl.BlockSpec(memory_space=pltpu.VMEM)
    out = pl.pallas_call(
        functools.partial(kernel, depth=depth, tp_count=tp_count, ctx_count=ctx_count),
        out_shape=jax.ShapeDtypeStruct((out_tokens, channels), BF),
        in_specs=[vmem, pl.BlockSpec(memory_space=pl.ANY)] + [vmem] * 6,
        out_specs=vmem,
        scratch_shapes=scratch,
        compiler_params=pltpu.CompilerParams(collective_id=0, has_side_effects=True, vmem_limit_bytes=60 * 2**20),
        name="hyena",
    )(
        activations,
        proj_weight,
        filter_taps.T,
        filter_blocks,
        skip_gain,
        jnp.asarray(forward),
        jnp.asarray(inverse),
        jnp.asarray(twiddle),
    )
    return out.T


def solution(mesh):
    placed = (P("ctx", "tp"), P("tp", None), P(None, ("ctx", "tp")), P(), P())
    return jax.shard_map(
        on_device, mesh=mesh, in_specs=placed, out_specs=P(None, ("ctx", "tp")), check_vma=False
    )
```

time: 83.4 us -> 69.3 us (0.83)
  Pallas kernels: 77 us -> 67.2 us
  local copies, waits for them, and re-layouts: 4.3 us -> 1.67 us
  other arithmetic: 1.77 us -> 0 us
    pallas_call x1, Pallas kernels: 77 us -> 67.2 us  [on_device(): pl.pallas_call(functools.partial(kernel, depth=depth, tp_count=tp_count,...]
    reshape x2 -> x0, local copies, waits for them, and re-layouts: 2.63 us -> none  [the longest x1 1.32 us: on_device(): filter_blocks.reshape(tp_count, width)]
    convert_element_type x1 -> x0, other arithmetic: 1.77 us -> none  [on_device(): filter_taps.T.astype(BF)]
where the time goes in v1:
time: 69.3 us; the launch traced here: 68.9 us
  Pallas kernels  67.2 us (97%)
  local copies, waits for them, and re-layouts  1.67 us (2%)
    pallas_call x1, Pallas kernels, on_device(): pl.pallas_call(functools.partial(kernel, depth=depth, tp_count=tp_count,...  67.2 us
    unnamed x1, local copies, waits for them, and re-layouts  1.67 us

profile of v1, /device:TPU:1, one launch (start us, length us, event | category | flops | bytes accessed | tf_op | source)
XLA Modules:
  0.0 68.9 jit_solution(17769871799095679172)
XLA Ops:
  0.0 67.2 %hyena.1 = bf16[32,4096]{1,0:T(8,128)(2,1)} custom-call(bf16[256,1024]{1,0:T(8,128)(2,1)} %act.1, bf16[1024,12288]{1,0:T(8,128)(2,1)} %weight.1, f32[32,4096]{1,0:T(8,128)} %bitcast.3, s32[4096]{0:T(1024)} %blocks.1, f32[4096]{0:T(1024)} %gains.1, bf16[2,256,256]{2,1,0:T(8,128)(2,1)} %constant.6.clone.forward, bf16[2,256,256]{2,1,0:T(8,128)(2,1)} %constant.7.clone.inverse, ...), custom_call_target="tpu_custom_call" | custom-call | tf_op jit(solution)/shard_map/hyena/pallas_call | solution.py:533
  67.2 1.7 %copy.10 = bf16[4096,32]{0,1:T(8,128)(2,1)} copy(bf16[4096,32]{0,1:T(8,128)(2,1)} %bitcast.2) | data formatting | bytes 524288

commit v2 on v1

--- a/solution.py
+++ b/solution.py
@@ -18,22 +18,25 @@
 SETS = 2
 SHIFT = 0.25
 
-ROWS_Z = 160
+ROWS_Z = 176
 LANES_Z = 2816
 
 SCHEDULE = (
-    ("mm", 0, 2), ("mm", 1, 2), ("bar",), ("x1", 0, 2), ("z1", 0, 0), ("tap",), ("z1", 0, 1), ("x1", 1, 2), ("mm", 0, 1),
-    ("mm", 0, 3), ("x1", 0, 1), ("z2f", 0, 0, 1), ("mm", 1, 1), ("mm", 1, 3), ("pz1", 0, 0, 0), ("z2f", 0, 1, 1), ("x1", 0, 3),
-    ("tx1", 0, 2), ("mm", 0, 0), ("x1", 0, 0), ("x2", 0), ("z2f", 1, 0, 0), ("z2f", 0, 0, 0), ("pz1", 0, 0, 1), ("z1", 1, 0),
-    ("x1", 1, 1), ("mm", 1, 0), ("tx1", 1, 2), ("mq", 0), ("mq", 1), ("pz1", 0, 1, 1), ("pz1", 0, 1, 0), ("zx", 0, 0), ("x2", 1),
-    ("z2f", 0, 1, 0), ("mask",), ("zx", 0, 1), ("tx1", 0, 3), ("x3f", 0, 1), ("px2", 0, 1), ("tx1", 0, 1), ("x3f", 0, 0),
-    ("px2", 0, 0), ("z2f", 1, 0, 1), ("mq", 2), ("pz1", 1, 0, 0), ("pz1", 1, 0, 1), ("x1", 1, 3), ("tx1", 1, 1), ("z1", 1, 1),
-    ("x1", 1, 0), ("mq", 3), ("px2", 1, 0), ("z2f", 1, 1, 1), ("x1", 2, 2), ("z2f", 2, 0, 0), ("filt",), ("fin", 0), ("gate", 0),
-    ("zx", 1, 1), ("zx", 1, 0), ("pz1", 1, 1, 0), ("pz1", 1, 1, 1), ("tx1", 1, 3), ("x3f", 1, 1), ("x1", 2, 1), ("px2", 1, 1),
-    ("z2f", 1, 1, 0), ("x3f", 1, 0), ("z1", 2, 0), ("z2f", 2, 0, 1), ("x1", 2, 3), ("tx1", 2, 2), ("z2f", 2, 1, 0), ("conv", 0),
-    ("fin", 1), ("gate", 1), ("pz1", 2, 0, 1), ("pz1", 2, 0, 0), ("tx1", 2, 1), ("x3f", 2, 0), ("x2", 2), ("tx1", 2, 3),
-    ("x3f", 2, 1), ("x1", 2, 0), ("z2f", 2, 1, 1), ("z1", 2, 1), ("home", 0), ("conv", 1), ("px2", 2, 0), ("px2", 2, 1),
-    ("zx", 2, 1), ("zx", 2, 0), ("pz1", 2, 1, 0), ("pz1", 2, 1, 1), ("home", 1), ("fin", 2), ("out",),
+    ("mm", 0, 2, 0), ("mm", 0, 2, 1), ("bar",), ("tap",), ("mm", 1, 2, 0), ("mm", 1, 2, 1), ("x1", 1, 2), ("z1", 0, 0),
+    ("x1", 0, 2), ("mm", 0, 1, 0), ("mm", 0, 1, 1), ("z1", 1, 0), ("mm", 0, 3, 0), ("mm", 0, 3, 1), ("z1", 0, 1), ("mm", 1, 1, 0),
+    ("mm", 1, 1, 1), ("x1", 0, 1), ("mm", 1, 3, 0), ("mm", 1, 3, 1), ("z2f", 0, 0, 1), ("x1", 1, 1), ("mm", 0, 0, 0),
+    ("mm", 0, 0, 1), ("x1", 0, 3), ("drain", 5), ("pz1", 0, 0, 1), ("pz1", 0, 0, 0), ("mask",), ("z2f", 0, 0, 0), ("x1", 1, 3),
+    ("mm", 1, 0, 0), ("mm", 1, 0, 1), ("tx1", 1, 2), ("z1", 1, 1), ("tx1", 0, 2), ("x2", 0), ("pz1", 1, 0, 1), ("drain", 16),
+    ("zx", 0, 0), ("mq", 0), ("mq", 1), ("tx1", 0, 1), ("x2", 1), ("z2f", 0, 1, 1), ("mq", 2), ("mq", 3), ("z2f", 1, 0, 0),
+    ("tx1", 0, 3), ("tx1", 1, 1), ("zx", 0, 1), ("x1", 1, 0), ("z2f", 1, 0, 1), ("pz1", 0, 1, 0), ("mq", 4), ("mq", 5),
+    ("drain", 22), ("px2", 1, 0), ("mq", 6), ("mq", 7), ("px2", 0, 1), ("pz1", 0, 1, 1), ("pz1", 1, 0, 0), ("x3f", 0, 1),
+    ("x3f", 0, 0), ("px2", 0, 0), ("tx1", 1, 3), ("z2f", 1, 1, 1), ("x1", 2, 2), ("z2f", 0, 1, 0), ("x1", 0, 0), ("filt",),
+    ("x3f", 1, 1), ("px2", 1, 1), ("z2f", 1, 1, 0), ("pz1", 1, 1, 1), ("x3f", 1, 0), ("zx", 1, 1), ("drain", 41), ("zx", 1, 0),
+    ("pz1", 1, 1, 0), ("x1", 2, 3), ("tx1", 2, 2), ("drain", 46), ("fin", 0), ("z1", 2, 0), ("z2f", 2, 0, 0), ("z1", 2, 1),
+    ("gate", 0), ("x1", 2, 1), ("drain", 60), ("fin", 1), ("gate", 1), ("x2", 2), ("z2f", 2, 1, 0), ("pz1", 2, 0, 0),
+    ("x1", 2, 0), ("pz1", 2, 0, 1), ("z2f", 2, 0, 1), ("drain", 64), ("conv", 0), ("tx1", 2, 3), ("pz1", 2, 1, 1), ("x3f", 2, 1),
+    ("z2f", 2, 1, 1), ("tx1", 2, 1), ("drain", 70), ("conv", 1), ("zx", 2, 1), ("pz1", 2, 1, 0), ("drain", 74), ("home", 0),
+    ("px2", 2, 0), ("zx", 2, 0), ("x3f", 2, 0), ("px2", 2, 1), ("drain", 82), ("home", 1), ("drain", 91), ("fin", 2), ("out",),
 )
 
 
@@ -200,6 +203,7 @@
     def __init__(self, send_sems, recv_sems):
         self.send_sems, self.recv_sems = send_sems, recv_sems
         self.used = 0
+        self.drained = 0
         self.started = []
 
     def make(self, src, dst, to, at):
@@ -219,6 +223,11 @@
         self.started.append(copy)
         return copy
 
+    def drain(self, count):
+        for at in range(self.drained, count):
+            self.started[at].wait_send()
+        self.drained = max(self.drained, count)
+
 
 class Swap:
     def __init__(self, links, count, me, device, src, dst):
@@ -235,6 +244,7 @@
 
     def start(self):
         self.each(lambda copy: copy.start())
+        self.links.started.append(self)
 
     def wait_recv(self):
         self.each(lambda copy: copy.wait_recv())
@@ -267,15 +277,16 @@
 
 
 def kernel(
-    act, weight, taps, blocks, gains, forward, inverse, twiddle,
+    act_hbm, weight, taps_hbm, blocks_hbm, gains_hbm, forward_hbm, inverse_hbm, twiddle_hbm,
     out,
+    act, taps, blocks, gains, forward, inverse, twiddle,
     wbuf, kv, qs,
     a_z1, a_z2, a_zx, a_x1, a_x2, a_x3,
     b_z1, b_z2, b_zx, b_x1, b_x2, b_x3,
     q_z1, q_z2, q_zx, q_x1, q_x2, q_x3,
     taps_out, taps_in, taps_t, filt_in, staged, filt_spec,
     gated, gated_t, gated_in, mixed, conv_out, conv_in, conv_home, conv_final,
-    w_sems, send_sems, recv_sems,
+    w_sems, in_sems, send_sems, recv_sems,
     *, depth, tp_count, ctx_count,
 ):
     place = Place(depth, tp_count, ctx_count)
@@ -289,9 +300,9 @@
 
     order = [step[1:] for step in SCHEDULE if step[0] == "mm"]
     tiles = []
-    for own, step in order:
-        base = place.owner(own, step) * width
-        tiles.append([(which * channels + base + c * piece, piece) for c in range(SETS) for which in (1, 2)])
+    for own, step, c in order:
+        base = place.owner(own, step) * width + c * piece
+        tiles.append([(which * channels + base, piece) for which in (1, 2)])
     for t in range(channels // tile):
         tiles.append([(t * tile, tile)])
 
@@ -299,30 +310,43 @@
         at = 0
         for k, (column, size) in enumerate(tiles[t]):
             src = weight.at[:, pl.ds(pl.multiple_of(column, size), size)]
-            act_on(pltpu.make_async_copy(src, wbuf.at[t, :, pl.ds(at, size)], w_sems.at[4 * t + k]))
+            act_on(pltpu.make_async_copy(src, wbuf.at[t, :, pl.ds(at, size)], w_sems.at[2 * t + k]))
             at += size
 
-    ahead = 4
-    for t in range(ahead):
+    barrier = pltpu.get_barrier_semaphore()
+
+    def greet(device):
+        pl.semaphore_signal(barrier, inc=1, device_id=device, device_id_type=pl.DeviceIdType.MESH)
+
+    greet(place.far)
+    for step in range(1, depth):
+        greet((me, place.owner(1, step)))
+    for step in range(1, depth):
+        greet((me, place.owner(0, step)))
+    for away in range(1, ctx_count):
+        greet(((me + away) % ctx_count, tp))
+
+    pairs = ((act_hbm, act), (taps_hbm, taps), (blocks_hbm, blocks), (gains_hbm, gains),
+             (forward_hbm, forward), (inverse_hbm, inverse), (twiddle_hbm, twiddle))
+    inputs = [pltpu.make_async_copy(source, target, in_sems.at[k]) for k, (source, target) in enumerate(pairs)]
+    inputs[0].start()
+    fetch(0, lambda copy: copy.start())
+    inputs[1].start()
+
+    ahead = 6
+    for t in range(1, ahead):
         fetch(t, lambda copy: copy.start())
+    for copy in inputs[2:]:
+        copy.start()
 
     def next_tile(t):
         fetch(t, lambda copy: copy.wait())
         if t + ahead < len(tiles):
             fetch(t + ahead, lambda copy: copy.start())
 
-    barrier = pltpu.get_barrier_semaphore()
-
-    def greet(device, count, mine):
-        def body(away, carry):
-            pl.semaphore_signal(barrier, inc=1, device_id=device((mine + away) % count), device_id_type=pl.DeviceIdType.MESH)
-            return carry
-        lax.fori_loop(1, count, body, 0)
-
-    greet(lambda peer: (me, peer), tp_count, tp)
-    greet(lambda peer: (peer, tp), ctx_count, me)
-
+    inputs[1].wait()
     taps_out[...] = taps[...].astype(BF)
+    inputs[0].wait()
 
     links = Links(send_sems, recv_sems)
 
@@ -358,10 +382,11 @@
         Spread(place, links, q_part, (q_z1, q_z2, q_zx, q_x1, q_x2, q_x3)),
     )
 
-    def multiply_kv(own, step):
-        t = order.index((own, step))
+    def multiply_kv(own, step, c):
+        t = order.index((own, step, c))
         next_tile(t)
-        kv[place.owner(own, step)] = jnp.dot(act[...], wbuf[t], preferred_element_type=F32).astype(BF)
+        block = jnp.dot(act[...], wbuf[t], preferred_element_type=F32)
+        kv[place.owner(own, step), :, pl.ds(c * tile, tile)] = block.astype(BF)
 
     def multiply_q(t):
         next_tile(len(order) + t)
@@ -371,6 +396,8 @@
     def mask():
         tap_swap.wait_recv()
         taps_in[span(tp, out_tokens), :] = taps_out[:, span(tp, width)]
+        for copy in inputs[2:]:
+            copy.wait()
         live = me < blocks[span(tp, width)].reshape(1, width)
         for c in range(SETS):
             for r in range(0, tokens, 128):
@@ -466,14 +493,12 @@
         "conv": convolve,
         "home": home,
         "out": finale,
+        "drain": links.drain,
     }
     for step in SCHEDULE:
         steps[step[0]](*step[1:])
 
-    for copy in links.started:
-        copy.wait_send()
-    for swap in [tap_swap, filt_swap] + gated_swap + conv_swap + home_swap:
-        swap.wait_send()
+    links.drain(len(links.started))
 
 
 def on_device(activations, proj_weight, filter_taps, filter_blocks, skip_gain):
@@ -494,7 +519,7 @@
             pltpu.VMEM((2, 2, x_rows, x_lanes), BF),
         ]
 
-    tile = 2 * width
+    tile = width
     n_tiles = 3 * channels // tile
     n_copies = (SETS + 1) * 28 + (1 + SETS) * (tp_count - 1) + (1 + 2 * SETS) * (ctx_count - 1)
     piece = width // SETS
@@ -502,6 +527,13 @@
     spec_rows = OUTER * lanes
     scratch = (
         [
+            pltpu.VMEM((tokens, depth_here), BF),
+            pltpu.VMEM((out_tokens, channels), F32),
+            pltpu.VMEM((channels,), jnp.int32),
+            pltpu.VMEM((channels,), F32),
+            pltpu.VMEM(forward.shape, BF),
+            pltpu.VMEM(inverse.shape, BF),
+            pltpu.VMEM(twiddle.shape, F32),
             pltpu.VMEM((n_tiles, depth_here, tile), BF),
             pltpu.VMEM((tp_count, tokens, 2 * width), BF),
             pltpu.VMEM((tp_count, out_tokens, channels), BF),
@@ -524,7 +556,8 @@
             pltpu.VMEM((SETS, piece, tokens), BF),
             pltpu.VMEM((SETS, tokens, piece), BF),
             pltpu.VMEM((SETS, tp_count, out_tokens, piece), BF),
-            pltpu.SemaphoreType.DMA((4 * n_tiles,)),
+            pltpu.SemaphoreType.DMA((2 * n_tiles,)),
+            pltpu.SemaphoreType.DMA((7,)),
             pltpu.SemaphoreType.DMA((n_copies,)),
             pltpu.SemaphoreType.DMA((n_copies,)),
         ]
@@ -533,7 +566,7 @@
     out = pl.pallas_call(
         functools.partial(kernel, depth=depth, tp_count=tp_count, ctx_count=ctx_count),
         out_shape=jax.ShapeDtypeStruct((out_tokens, channels), BF),
-        in_specs=[vmem, pl.BlockSpec(memory_space=pl.ANY)] + [vmem] * 6,
+        in_specs=[pl.BlockSpec(memory_space=pl.ANY)] * 8,
         out_specs=vmem,
         scratch_shapes=scratch,
         compiler_params=pltpu.CompilerParams(collective_id=0, has_side_effects=True, vmem_limit_bytes=60 * 2**20),

time: 69.3 us -> 66.1 us (0.954)
  Pallas kernels: 67.2 us -> 63.9 us
    pallas_call x1, Pallas kernels: 67.2 us -> 63.9 us  [on_device(): pl.pallas_call(functools.partial(kernel, depth=depth, tp_count=tp_count,...]
where the time goes in v2:
time: 66.1 us; the launch traced here: 65.6 us
  Pallas kernels  63.9 us (97%)
  local copies, waits for them, and re-layouts  1.67 us (3%)
    pallas_call x1, Pallas kernels, on_device(): pl.pallas_call(functools.partial(kernel, depth=depth, tp_count=tp_count,...  63.9 us
    unnamed x1, local copies, waits for them, and re-layouts  1.67 us

profile of v2, /device:TPU:1, one launch (start us, length us, event | category | flops | bytes accessed | tf_op | source)
XLA Modules:
  0.0 65.6 jit_solution(7281829706407040167)
XLA Ops:
  0.0 63.9 %hyena.1 = bf16[32,4096]{1,0:T(8,128)(2,1)} custom-call(bf16[256,1024]{1,0:T(8,128)(2,1)} %act_hbm.1, bf16[1024,12288]{1,0:T(8,128)(2,1)} %weight.1, f32[32,4096]{1,0:T(8,128)} %bitcast.3, s32[4096]{0:T(1024)} %blocks_hbm.1, f32[4096]{0:T(1024)} %gains_hbm.1, bf16[2,256,256]{2,1,0:T(8,128)(2,1)} %constant.6.clone.forward_hbm, ...), custom_call_target="tpu_custom_call" | custom-call | tf_op jit(solution)/shard_map/hyena/pallas_call | solution.py:566
  63.9 1.7 %copy.10 = bf16[4096,32]{0,1:T(8,128)(2,1)} copy(bf16[4096,32]{0,1:T(8,128)(2,1)} %bitcast.2) | data formatting | bytes 524288

commit v3 on v2

--- a/solution.py
+++ b/solution.py
@@ -15,28 +15,30 @@
 OUTER = 32
 INNER = 128
 LENGTH = OUTER * INNER
+SIDES = 2
 SETS = 2
 SHIFT = 0.25
 
-ROWS_Z = 176
-LANES_Z = 2816
+ROWS_Z = 160
+LANES_Z = 2560
 
 SCHEDULE = (
-    ("mm", 0, 2, 0), ("mm", 0, 2, 1), ("bar",), ("tap",), ("mm", 1, 2, 0), ("mm", 1, 2, 1), ("x1", 1, 2), ("z1", 0, 0),
-    ("x1", 0, 2), ("mm", 0, 1, 0), ("mm", 0, 1, 1), ("z1", 1, 0), ("mm", 0, 3, 0), ("mm", 0, 3, 1), ("z1", 0, 1), ("mm", 1, 1, 0),
-    ("mm", 1, 1, 1), ("x1", 0, 1), ("mm", 1, 3, 0), ("mm", 1, 3, 1), ("z2f", 0, 0, 1), ("x1", 1, 1), ("mm", 0, 0, 0),
-    ("mm", 0, 0, 1), ("x1", 0, 3), ("drain", 5), ("pz1", 0, 0, 1), ("pz1", 0, 0, 0), ("mask",), ("z2f", 0, 0, 0), ("x1", 1, 3),
-    ("mm", 1, 0, 0), ("mm", 1, 0, 1), ("tx1", 1, 2), ("z1", 1, 1), ("tx1", 0, 2), ("x2", 0), ("pz1", 1, 0, 1), ("drain", 16),
-    ("zx", 0, 0), ("mq", 0), ("mq", 1), ("tx1", 0, 1), ("x2", 1), ("z2f", 0, 1, 1), ("mq", 2), ("mq", 3), ("z2f", 1, 0, 0),
-    ("tx1", 0, 3), ("tx1", 1, 1), ("zx", 0, 1), ("x1", 1, 0), ("z2f", 1, 0, 1), ("pz1", 0, 1, 0), ("mq", 4), ("mq", 5),
-    ("drain", 22), ("px2", 1, 0), ("mq", 6), ("mq", 7), ("px2", 0, 1), ("pz1", 0, 1, 1), ("pz1", 1, 0, 0), ("x3f", 0, 1),
-    ("x3f", 0, 0), ("px2", 0, 0), ("tx1", 1, 3), ("z2f", 1, 1, 1), ("x1", 2, 2), ("z2f", 0, 1, 0), ("x1", 0, 0), ("filt",),
-    ("x3f", 1, 1), ("px2", 1, 1), ("z2f", 1, 1, 0), ("pz1", 1, 1, 1), ("x3f", 1, 0), ("zx", 1, 1), ("drain", 41), ("zx", 1, 0),
-    ("pz1", 1, 1, 0), ("x1", 2, 3), ("tx1", 2, 2), ("drain", 46), ("fin", 0), ("z1", 2, 0), ("z2f", 2, 0, 0), ("z1", 2, 1),
-    ("gate", 0), ("x1", 2, 1), ("drain", 60), ("fin", 1), ("gate", 1), ("x2", 2), ("z2f", 2, 1, 0), ("pz1", 2, 0, 0),
-    ("x1", 2, 0), ("pz1", 2, 0, 1), ("z2f", 2, 0, 1), ("drain", 64), ("conv", 0), ("tx1", 2, 3), ("pz1", 2, 1, 1), ("x3f", 2, 1),
-    ("z2f", 2, 1, 1), ("tx1", 2, 1), ("drain", 70), ("conv", 1), ("zx", 2, 1), ("pz1", 2, 1, 0), ("drain", 74), ("home", 0),
-    ("px2", 2, 0), ("zx", 2, 0), ("x3f", 2, 0), ("px2", 2, 1), ("drain", 82), ("home", 1), ("drain", 91), ("fin", 2), ("out",),
+    ("mm", 0, 3, 0), ("mm", 1, 2, 1), ("mm", 0, 2, 0), ("bar",), ("tap",), ("mm", 0, 3, 1), ("mm", 0, 2, 1), ("z1", 1, 1),
+    ("mm", 0, 0, 1), ("x1", 0, 3), ("mm", 1, 2, 0), ("z1", 0, 0), ("x1", 1, 0), ("z2f", 0, 0, 1), ("mm", 0, 1, 0), ("z1", 1, 0),
+    ("mm", 0, 0, 0), ("mm", 0, 1, 1), ("x1", 0, 2), ("mm", 1, 3, 0), ("z2f", 1, 0, 0), ("z2f", 1, 0, 1), ("x1", 1, 2),
+    ("mm", 1, 0, 0), ("z1", 0, 1), ("mm", 1, 1, 0), ("mask",), ("x1", 0, 1), ("z2f", 0, 0, 0), ("mm", 1, 0, 1), ("x1", 1, 3),
+    ("mm", 1, 3, 1), ("drain", 7), ("pz1", 0, 0, 1), ("pz1", 1, 0, 0), ("tx1", 0, 3), ("x3f", 0, 1), ("x1", 1, 1),
+    ("mm", 1, 1, 1), ("x1", 0, 0), ("pz1", 1, 1, 1), ("pz1", 0, 0, 0), ("mq", 0), ("tx1", 0, 2), ("x2", 0), ("mq", 1),
+    ("drain", 18), ("tx1", 1, 2), ("x2", 1), ("pz1", 1, 1, 0), ("drain", 24), ("tx1", 0, 1), ("pz1", 1, 0, 1), ("mq", 2),
+    ("pz1", 0, 1, 0), ("z2f", 0, 1, 0), ("mq", 3), ("mq", 4), ("zx", 1, 0), ("mq", 5), ("drain", 29), ("zx", 0, 0),
+    ("pz1", 0, 1, 1), ("zx", 0, 1), ("tx1", 1, 3), ("z2f", 0, 1, 1), ("filt",), ("z2f", 1, 1, 0), ("mq", 6), ("tx1", 1, 1),
+    ("x3f", 0, 0), ("px2", 0, 0), ("px2", 0, 1), ("px2", 1, 1), ("drain", 42), ("zx", 1, 1), ("mq", 7), ("px2", 1, 0),
+    ("x1", 2, 3), ("x3f", 1, 1), ("z2f", 1, 1, 1), ("x1", 2, 2), ("x3f", 1, 0), ("z1", 2, 0), ("z1", 2, 1), ("z2f", 2, 0, 0),
+    ("z2f", 2, 0, 1), ("drain", 54), ("fin", 0), ("gate", 0), ("drain", 62), ("fin", 1), ("gate", 1), ("x1", 2, 1),
+    ("pz1", 2, 0, 1), ("x1", 2, 0), ("tx1", 2, 2), ("pz1", 2, 0, 0), ("x2", 2), ("tx1", 2, 3), ("z2f", 2, 1, 1), ("drain", 66),
+    ("pz1", 2, 1, 0), ("z2f", 2, 1, 0), ("conv", 0), ("drain", 70), ("conv", 1), ("zx", 2, 1), ("x3f", 2, 1), ("tx1", 2, 1),
+    ("x3f", 2, 0), ("zx", 2, 0), ("pz1", 2, 1, 1), ("drain", 80), ("home", 0), ("px2", 2, 0), ("px2", 2, 1), ("drain", 86),
+    ("home", 1), ("drain", 91), ("fin", 2), ("out",),
 )
 
 
@@ -260,13 +262,9 @@
             target[pl.ds(c, 128), pl.ds(r, 128)] = tile.T.astype(target.dtype)
 
 
-def spectrum(source, staged, twiddle):
-    ctx_count, lanes, span = source.shape
-    blocks = []
-    for i in range(ctx_count):
-        for u in range(span // INNER):
-            blocks.append(source[i, :, pl.ds(u * INNER, INNER)].astype(F32))
-    for f, (re, im) in enumerate(outer_forward(blocks)):
+def spectrum(blocks, staged, twiddle):
+    lanes = blocks[0].shape[0]
+    for f, (re, im) in enumerate(outer_forward([block.astype(F32) for block in blocks])):
         c, s = twiddle[0, pl.ds(f, 1), :], twiddle[1, pl.ds(f, 1), :]
         staged[pl.ds(f * lanes, lanes), pl.ds(0, INNER)] = (re * c + im * s).astype(BF)
         staged[pl.ds(f * lanes, lanes), pl.ds(INNER, INNER)] = (im * c - re * s).astype(BF)
@@ -284,7 +282,7 @@
     a_z1, a_z2, a_zx, a_x1, a_x2, a_x3,
     b_z1, b_z2, b_zx, b_x1, b_x2, b_x3,
     q_z1, q_z2, q_zx, q_x1, q_x2, q_x3,
-    taps_out, taps_in, taps_t, filt_in, staged, filt_spec,
+    taps_out, taps_in, taps_t, filt_in, staged, filt_spec, gain_t,
     gated, gated_t, gated_in, mixed, conv_out, conv_in, conv_home, conv_final,
     w_sems, in_sems, send_sems, recv_sems,
     *, depth, tp_count, ctx_count,
@@ -297,12 +295,16 @@
     tile = wbuf.shape[2]
     piece = width // SETS
     lanes = piece // ctx_count
+    spots = ctx_count // SIDES
+    part = lanes * spots
+    side, spot = me // spots, me % spots
+    crowd = SIDES * tp_count
 
     order = [step[1:] for step in SCHEDULE if step[0] == "mm"]
     tiles = []
     for own, step, c in order:
-        base = place.owner(own, step) * width + c * piece
-        tiles.append([(which * channels + base, piece) for which in (1, 2)])
+        base = place.owner(own, step) * width + c * part
+        tiles.append([(which * channels + base + side * piece, part) for which in (1, 2) for side in range(SIDES)])
     for t in range(channels // tile):
         tiles.append([(t * tile, tile)])
 
@@ -310,7 +312,7 @@
         at = 0
         for k, (column, size) in enumerate(tiles[t]):
             src = weight.at[:, pl.ds(pl.multiple_of(column, size), size)]
-            act_on(pltpu.make_async_copy(src, wbuf.at[t, :, pl.ds(at, size)], w_sems.at[2 * t + k]))
+            act_on(pltpu.make_async_copy(src, wbuf.at[t, :, pl.ds(at, size)], w_sems.at[4 * t + k]))
             at += size
 
     barrier = pltpu.get_barrier_semaphore()
@@ -318,13 +320,29 @@
     def greet(device):
         pl.semaphore_signal(barrier, inc=1, device_id=device, device_id_type=pl.DeviceIdType.MESH)
 
+    def across(away):
+        return (me + away) % ctx_count
+
+    other = (me + spots) % ctx_count
+    half = spots // 2
+    greet((me, place.owner(0, 2)))
+    for away in (spots + half + 1, spots + half, spots + half - 1):
+        greet((across(away), tp))
+    for own in (0, 1):
+        greet((other, place.owner(own, 2)))
+    for step in (1, 3):
+        greet((me, place.owner(0, step)))
+    greet((me, place.owner(1, 2)))
+    for away in range(1, ctx_count):
+        if away not in (spots + half + 1, spots + half, spots + half - 1):
+            greet((across(away), tp))
+    for step in (1, 3):
+        for own in (0, 1):
+            greet((other, place.owner(own, step)))
+    greet((other, place.owner(0, 0)))
+    for step in (1, 3):
+        greet((me, place.owner(1, step)))
     greet(place.far)
-    for step in range(1, depth):
-        greet((me, place.owner(1, step)))
-    for step in range(1, depth):
-        greet((me, place.owner(0, step)))
-    for away in range(1, ctx_count):
-        greet(((me + away) % ctx_count, tp))
 
     pairs = ((act_hbm, act), (taps_hbm, taps), (blocks_hbm, blocks), (gains_hbm, gains),
              (forward_hbm, forward), (inverse_hbm, inverse), (twiddle_hbm, twiddle))
@@ -344,14 +362,16 @@
         if t + ahead < len(tiles):
             fetch(t + ahead, lambda copy: copy.start())
 
-    inputs[1].wait()
-    taps_out[...] = taps[...].astype(BF)
     inputs[0].wait()
 
     links = Links(send_sems, recv_sems)
 
-    def over_tp(src, dst):
-        return Swap(links, tp_count, tp, lambda peer: (me, peer), src, dst)
+    def over_crowd(src, dst):
+        device = lambda peer: (peer // tp_count * spots + spot, peer % tp_count)
+        return Swap(links, crowd, side * tp_count + tp, device, src, dst)
+
+    def over_side(src, dst):
+        return Swap(links, spots, spot, lambda peer: (side * spots + peer, tp), src, dst)
 
     def over_ctx(src, dst):
         return Swap(links, ctx_count, me, lambda peer: (peer, tp), src, dst)
@@ -359,11 +379,20 @@
     def span(index, size):
         return pl.ds(pl.multiple_of(index * size, size), size)
 
-    tap_swap = over_tp(lambda peer: taps_out.at[:, span(peer, width)], lambda mine: taps_in.at[span(mine, out_tokens)])
-    filt_swap = over_ctx(lambda peer: taps_t.at[:, span(peer, lanes)], lambda mine: filt_in.at[mine])
-    gated_swap = [over_ctx(lambda peer, c=c: gated_t.at[c, span(peer, lanes)], lambda mine, c=c: gated_in.at[c, mine]) for c in range(SETS)]
-    conv_swap = [over_ctx(lambda peer, c=c: conv_out.at[c, peer], lambda mine, c=c: conv_in.at[c, span(mine, lanes)]) for c in range(SETS)]
-    home_swap = [over_tp(lambda peer, c=c: conv_home.at[c, span(peer, out_tokens)], lambda mine, c=c: conv_final.at[c, mine]) for c in range(SETS)]
+    tap_swap = over_crowd(
+        lambda peer: taps_out.at[:, span(peer % tp_count * SIDES + peer // tp_count, piece)], lambda mine: taps_in.at[mine]
+    )
+    filt_swap = over_side(lambda peer: taps_t.at[:, span(peer, lanes)], lambda mine: filt_in.at[mine])
+    gated_swap, conv_swap, home_swap = [], [], []
+    for c in range(SETS):
+        gated_swap.append(over_ctx(lambda peer, c=c: gated_t.at[c, span(peer, lanes)], lambda mine, c=c: gated_in.at[c, mine]))
+        conv_swap.append(over_side(lambda peer, c=c: conv_out.at[c, peer], lambda mine, c=c: conv_in.at[c, span(mine, lanes)]))
+        home_swap.append(over_crowd(lambda peer, c=c: conv_home.at[c, span(peer, out_tokens)], lambda mine, c=c: conv_final.at[c, mine]))
+
+    def send_taps():
+        inputs[1].wait()
+        taps_out[...] = taps[...].astype(BF)
+        tap_swap.start()
 
     def kv_part(c):
         def part(owner, which, half):
@@ -394,27 +423,34 @@
         qs[:, :, pl.ds(t * tile, tile)] = block.reshape(tp_count, out_tokens, tile)
 
     def mask():
-        tap_swap.wait_recv()
-        taps_in[span(tp, out_tokens), :] = taps_out[:, span(tp, width)]
         for copy in inputs[2:]:
             copy.wait()
-        live = me < blocks[span(tp, width)].reshape(1, width)
+        tap_swap.wait_recv()
+        taps_in[side * tp_count + tp] = taps_out[:, span(tp * SIDES + side, piece)]
         for c in range(SETS):
-            for r in range(0, tokens, 128):
-                for k in range(0, piece, 128):
-                    at = c * piece + k
-                    block = taps_in[pl.ds(r, 128), pl.ds(at, 128)].astype(F32)
-                    block = jnp.where(live[:, at:at + 128], block, 0.0)
-                    taps_t[c, pl.ds(k, 128), pl.ds(r, 128)] = block.T.astype(BF)
+            at = span((tp * SIDES + side) * SETS + c, part)
+            depth_of = blocks[at].reshape(1, part)
+            gain_t[c] = jnp.broadcast_to(gains[at].reshape(1, part), (part, part)).T
+            for n in range(crowd * out_tokens // INNER):
+                per = INNER // out_tokens
+                block = taps_in[pl.ds(n * per, per), :, pl.ds(c * part, part)].reshape(INNER, part).astype(F32)
+                index = n * INNER // tokens * spots + spot
+                taps_t[c, :, pl.ds(n * INNER, INNER)] = jnp.where(index < depth_of, block, 0.0).T.astype(BF)
         filt_swap.start()
 
     rows = staged.shape[1] // 2
+
+    fold = tokens // INNER
 
     def filter_spectrum():
         filt_swap.wait_recv()
-        filt_in[me] = taps_t[:, span(me, lanes), :]
+        filt_in[spot] = taps_t[:, span(spot, lanes), :]
         for c in range(SETS):
-            spectrum(filt_in.at[:, c], staged.at[c], twiddle)
+            parts = []
+            for a in range(OUTER):
+                i, u = a // fold, a % fold
+                parts.append(filt_in[i % spots, c, :, pl.ds((i // spots * fold + u) * INNER, INNER)])
+            spectrum(parts, staged.at[c], twiddle)
             for n in range(2):
                 at = pl.ds(n * rows, rows)
                 filt_spec[c, at, :] = both(staged[c, at, :], forward)
@@ -432,7 +468,8 @@
     def convolve(c):
         gated_swap[c].wait_recv()
         gated_in[c, me] = gated_t[c, span(me, lanes), :]
-        spectrum(gated_in.at[c], staged.at[c], twiddle)
+        parts = [gated_in[c, a // fold, :, pl.ds(a % fold * INNER, INNER)] for a in range(OUTER)]
+        spectrum(parts, staged.at[c], twiddle)
         for n in range(2):
             at = pl.ds(n * rows, rows)
             a, b = both(staged[c, at, :], forward), filt_spec[c, at, :]
@@ -445,38 +482,34 @@
             row = pl.ds(f * lanes, lanes)
             re, im = mixed[row, pl.ds(0, INNER)], mixed[row, pl.ds(INNER, INNER)]
             data.append((re * cos - im * sin, re * sin + im * cos))
-        fold = tokens // INNER
+        gain = gain_t[c, span(spot, lanes), :]
         for a, block in enumerate(outer_inverse(data)):
-            conv_out[c, a // fold, :, pl.ds(a % fold * INNER, INNER)] = block.astype(BF)
+            i, u = a // fold, a % fold
+            at = pl.ds((i // spots * fold + u) * INNER, INNER)
+            conv_out[c, i % spots, :, at] = (block + gain * parts[a].astype(F32)).astype(BF)
         conv_swap[c].start()
 
     def home(c):
         conv_swap[c].wait_recv()
-        conv_in[c, span(me, lanes), :] = conv_out[c, me]
-        gain = gains[span(tp, width)].reshape(1, width)
-        for r in range(0, tokens, 128):
-            for k in range(0, piece, 128):
-                at = c * piece + k
-                conv = conv_in[c, pl.ds(k, 128), pl.ds(r, 128)].astype(F32).T
-                total = conv + gain[:, at:at + 128] * gated[pl.ds(r, 128), pl.ds(at, 128)]
-                conv_home[c, pl.ds(r, 128), pl.ds(k, 128)] = total.astype(BF)
+        conv_in[c, span(spot, lanes), :] = conv_out[c, spot]
+        transposed(conv_in.at[c], conv_home.at[c], part, SIDES * tokens)
         home_swap[c].start()
 
     def finale():
-        for c in range(SETS):
+        query = jnp.concatenate([spreads[SETS].total(which, half) for which in (0, 1) for half in (0, 1)], axis=1)
+        for c in [step[1] for step in SCHEDULE if step[0] == "home"]:
             home_swap[c].wait_recv()
-            conv_final[c, tp] = conv_home[c, span(tp, out_tokens), :]
-        query = jnp.concatenate([spreads[SETS].total(which, half) for which in (0, 1) for half in (0, 1)], axis=1)
-        for j in range(tp_count):
-            for c in range(SETS):
-                at = slice(j * width + c * piece, j * width + (c + 1) * piece)
-                out[:, at] = (query[:, at] * conv_final[c, j].astype(F32)).astype(BF)
+            conv_final[c, side * tp_count + tp] = conv_home[c, span(side * tp_count + tp, out_tokens), :]
+            for peer in range(crowd):
+                first = ((peer % tp_count * SIDES + peer // tp_count) * SETS + c) * part
+                at = slice(first, first + part)
+                out[:, at] = (query[:, at] * conv_final[c, peer].astype(F32)).astype(BF)
 
     steps = {
-        "bar": lambda: pl.semaphore_wait(barrier, tp_count + ctx_count - 2),
+        "bar": lambda: pl.semaphore_wait(barrier, 2 * tp_count + ctx_count - 3),
         "mm": multiply_kv,
         "mq": multiply_q,
-        "tap": tap_swap.start,
+        "tap": send_taps,
         "mask": mask,
         "filt": filter_spectrum,
         "z1": lambda c, own: spreads[c].start_z1(own),
@@ -521,9 +554,12 @@
 
     tile = width
     n_tiles = 3 * channels // tile
-    n_copies = (SETS + 1) * 28 + (1 + SETS) * (tp_count - 1) + (1 + 2 * SETS) * (ctx_count - 1)
+    n_copies = (SETS + 1) * 28 + (1 + SETS) * (2 * tp_count + ctx_count // SIDES - 2) + SETS * (ctx_count - 1)
     piece = width // SETS
     lanes = piece // ctx_count
+    spots = ctx_count // SIDES
+    part = lanes * spots
+    crowd = SIDES * tp_count
     spec_rows = OUTER * lanes
     scratch = (
         [
@@ -543,20 +579,21 @@
         + buffers(out_tokens, LANES_Z // 2, out_tokens, (channels - LANES_Z) // 2)
         + [
             pltpu.VMEM((out_tokens, channels), BF),
-            pltpu.VMEM((tokens, width), BF),
-            pltpu.VMEM((SETS, piece, tokens), BF),
-            pltpu.VMEM((ctx_count, SETS, lanes, tokens), BF),
+            pltpu.VMEM((crowd, out_tokens, piece), BF),
+            pltpu.VMEM((SETS, part, SIDES * tokens), BF),
+            pltpu.VMEM((spots, SETS, lanes, SIDES * tokens), BF),
             pltpu.VMEM((SETS, spec_rows, 2 * INNER), BF),
             pltpu.VMEM((SETS, spec_rows, 2 * INNER), F32),
+            pltpu.VMEM((SETS, part, part), F32),
             pltpu.VMEM((tokens, width), F32),
             pltpu.VMEM((SETS, piece, tokens), BF),
             pltpu.VMEM((SETS, ctx_count, lanes, tokens), BF),
             pltpu.VMEM((spec_rows, 2 * INNER), F32),
-            pltpu.VMEM((SETS, ctx_count, lanes, tokens), BF),
-            pltpu.VMEM((SETS, piece, tokens), BF),
-            pltpu.VMEM((SETS, tokens, piece), BF),
-            pltpu.VMEM((SETS, tp_count, out_tokens, piece), BF),
-            pltpu.SemaphoreType.DMA((2 * n_tiles,)),
+            pltpu.VMEM((SETS, spots, lanes, SIDES * tokens), BF),
+            pltpu.VMEM((SETS, part, SIDES * tokens), BF),
+            pltpu.VMEM((SETS, SIDES * tokens, part), BF),
+            pltpu.VMEM((SETS, crowd, out_tokens, part), BF),
+            pltpu.SemaphoreType.DMA((4 * n_tiles,)),
             pltpu.SemaphoreType.DMA((7,)),
             pltpu.SemaphoreType.DMA((n_copies,)),
             pltpu.SemaphoreType.DMA((n_copies,)),
@@ -565,7 +602,7 @@
     vmem = pl.BlockSpec(memory_space=pltpu.VMEM)
     out = pl.pallas_call(
         functools.partial(kernel, depth=depth, tp_count=tp_count, ctx_count=ctx_count),
-        out_shape=jax.ShapeDtypeStruct((out_tokens, channels), BF),
+        out_shape=pltpu.VMEM((out_tokens, channels), BF),
         in_specs=[pl.BlockSpec(memory_space=pl.ANY)] * 8,
         out_specs=vmem,
         scratch_shapes=scratch,

time: 66.1 us -> 62.6 us (0.947)
  Pallas kernels: 63.9 us -> 61.8 us
  local copies, waits for them, and re-layouts: 1.67 us -> 0.71 us
    pallas_call x1, Pallas kernels: 63.9 us -> 61.8 us  [on_device(): pl.pallas_call(functools.partial(kernel, depth=depth, tp_count=tp_count,...]
    unnamed x1, local copies, waits for them, and re-layouts: 1.67 us -> 0.71 us
where the time goes in v3:
time: 62.6 us; the launch traced here: 62.5 us
  Pallas kernels  61.8 us (99%)
  local copies, waits for them, and re-layouts  0.71 us (1%)
    pallas_call x1, Pallas kernels, on_device(): pl.pallas_call(functools.partial(kernel, depth=depth, tp_count=tp_count,...  61.8 us

profile of v3, /device:TPU:1, one launch (start us, length us, event | category | flops | bytes accessed | tf_op | source)
XLA Modules:
  0.0 62.5 jit_solution(12738484995006457100)
XLA Ops:
  0.0 61.8 %hyena.1 = bf16[32,4096]{1,0:T(8,128)(2,1)S(1)} custom-call(bf16[256,1024]{1,0:T(8,128)(2,1)} %act_hbm.1, bf16[1024,12288]{1,0:T(8,128)(2,1)} %weight.1, f32[32,4096]{1,0:T(8,128)} %bitcast.3, s32[4096]{0:T(1024)} %blocks_hbm.1, f32[4096]{0:T(1024)} %gains_hbm.1, bf16[2,256,256]{2,1,0:T(8,128)(2,1)} %constant.6.clone.forward_hbm, ...), custom_call_target="tpu_custom_call" | custom-call | tf_op jit(solution)/shard_map/hyena/pallas_call | solution.py:603
  61.8 0.7 %copy.10 = bf16[4096,32]{0,1:T(8,128)(2,1)} copy(bf16[4096,32]{0,1:T(8,128)(2,1)S(1)} %bitcast.2) | data formatting | bytes 524288

commit v4 on v3

--- a/solution.py
+++ b/solution.py
@@ -30,15 +30,15 @@
     ("mm", 1, 3, 1), ("drain", 7), ("pz1", 0, 0, 1), ("pz1", 1, 0, 0), ("tx1", 0, 3), ("x3f", 0, 1), ("x1", 1, 1),
     ("mm", 1, 1, 1), ("x1", 0, 0), ("pz1", 1, 1, 1), ("pz1", 0, 0, 0), ("mq", 0), ("tx1", 0, 2), ("x2", 0), ("mq", 1),
     ("drain", 18), ("tx1", 1, 2), ("x2", 1), ("pz1", 1, 1, 0), ("drain", 24), ("tx1", 0, 1), ("pz1", 1, 0, 1), ("mq", 2),
-    ("pz1", 0, 1, 0), ("z2f", 0, 1, 0), ("mq", 3), ("mq", 4), ("zx", 1, 0), ("mq", 5), ("drain", 29), ("zx", 0, 0),
+    ("pz1", 0, 1, 0), ("drain", 29), ("zx", 0, 0), ("z2f", 0, 1, 0), ("mq", 3), ("mq", 4), ("zx", 1, 0), ("mq", 5),
     ("pz1", 0, 1, 1), ("zx", 0, 1), ("tx1", 1, 3), ("z2f", 0, 1, 1), ("filt",), ("z2f", 1, 1, 0), ("mq", 6), ("tx1", 1, 1),
-    ("x3f", 0, 0), ("px2", 0, 0), ("px2", 0, 1), ("px2", 1, 1), ("drain", 42), ("zx", 1, 1), ("mq", 7), ("px2", 1, 0),
-    ("x1", 2, 3), ("x3f", 1, 1), ("z2f", 1, 1, 1), ("x1", 2, 2), ("x3f", 1, 0), ("z1", 2, 0), ("z1", 2, 1), ("z2f", 2, 0, 0),
-    ("z2f", 2, 0, 1), ("drain", 54), ("fin", 0), ("gate", 0), ("drain", 62), ("fin", 1), ("gate", 1), ("x1", 2, 1),
-    ("pz1", 2, 0, 1), ("x1", 2, 0), ("tx1", 2, 2), ("pz1", 2, 0, 0), ("x2", 2), ("tx1", 2, 3), ("z2f", 2, 1, 1), ("drain", 66),
-    ("pz1", 2, 1, 0), ("z2f", 2, 1, 0), ("conv", 0), ("drain", 70), ("conv", 1), ("zx", 2, 1), ("x3f", 2, 1), ("tx1", 2, 1),
-    ("x3f", 2, 0), ("zx", 2, 0), ("pz1", 2, 1, 1), ("drain", 80), ("home", 0), ("px2", 2, 0), ("px2", 2, 1), ("drain", 86),
-    ("home", 1), ("drain", 91), ("fin", 2), ("out",),
+    ("x3f", 0, 0), ("px2", 0, 0), ("px2", 0, 1), ("px2", 1, 1), ("zx", 1, 1), ("mq", 7), ("px2", 1, 0), ("x1", 2, 3),
+    ("x3f", 1, 1), ("z2f", 1, 1, 1), ("x1", 2, 2), ("x3f", 1, 0), ("z1", 2, 0), ("z1", 2, 1), ("z2f", 2, 0, 0), ("z2f", 2, 0, 1),
+    ("drain", 54), ("fin", 0), ("gate", 0), ("drain", 59), ("fin", 1), ("gate", 1), ("x1", 2, 1), ("pz1", 2, 0, 1), ("x1", 2, 0),
+    ("z2f", 2, 1, 1), ("tx1", 2, 2), ("pz1", 2, 0, 0), ("x2", 2), ("tx1", 2, 3), ("drain", 66), ("pz1", 2, 1, 0),
+    ("z2f", 2, 1, 0), ("conv", 0), ("drain", 70), ("conv", 1), ("zx", 2, 1), ("x3f", 2, 1), ("tx1", 2, 1), ("x3f", 2, 0),
+    ("zx", 2, 0), ("pz1", 2, 1, 1), ("drain", 80), ("home", 0), ("px2", 2, 0), ("px2", 2, 1), ("drain", 86), ("home", 1),
+    ("drain", 91), ("fin", 2), ("out",),
 )
 
 
@@ -349,12 +349,11 @@
     inputs = [pltpu.make_async_copy(source, target, in_sems.at[k]) for k, (source, target) in enumerate(pairs)]
     inputs[0].start()
     fetch(0, lambda copy: copy.start())
-    inputs[1].start()
-
-    ahead = 6
+
+    ahead = 4
     for t in range(1, ahead):
         fetch(t, lambda copy: copy.start())
-    for copy in inputs[2:]:
+    for copy in inputs[1:]:
         copy.start()
 
     def next_tile(t):

time: 62.6 us -> 62 us (level)
  Pallas kernels: 61.8 us -> 61.1 us
    pallas_call x1, Pallas kernels: 61.8 us -> 61.1 us  [on_device(): pl.pallas_call(functools.partial(kernel, depth=depth, tp_count=tp_count,...]
where the time goes in v4:
time: 62 us; the launch traced here: 61.9 us
  Pallas kernels  61.1 us (99%)
  local copies, waits for them, and re-layouts  0.71 us (1%)
    pallas_call x1, Pallas kernels, on_device(): pl.pallas_call(functools.partial(kernel, depth=depth, tp_count=tp_count,...  61.1 us

profile of v4, /device:TPU:1, one launch (start us, length us, event | category | flops | bytes accessed | tf_op | source)
XLA Modules:
  0.0 61.9 jit_solution(6778003136658345734)
XLA Ops:
  0.0 61.1 %hyena.1 = bf16[32,4096]{1,0:T(8,128)(2,1)S(1)} custom-call(bf16[256,1024]{1,0:T(8,128)(2,1)} %act_hbm.1, bf16[1024,12288]{1,0:T(8,128)(2,1)} %weight.1, f32[32,4096]{1,0:T(8,128)} %bitcast.3, s32[4096]{0:T(1024)} %blocks_hbm.1, f32[4096]{0:T(1024)} %gains_hbm.1, bf16[2,256,256]{2,1,0:T(8,128)(2,1)} %constant.6.clone.forward_hbm, ...), custom_call_target="tpu_custom_call" | custom-call | tf_op jit(solution)/shard_map/hyena/pallas_call | solution.py:602
  61.2 0.7 %copy.10 = bf16[4096,32]{0,1:T(8,128)(2,1)} copy(bf16[4096,32]{0,1:T(8,128)(2,1)S(1)} %bitcast.2) | data formatting | bytes 524288

commit v5 on v4

--- a/solution.py
+++ b/solution.py
@@ -471,10 +471,11 @@
         spectrum(parts, staged.at[c], twiddle)
         for n in range(2):
             at = pl.ds(n * rows, rows)
-            a, b = both(staged[c, at, :], forward), filt_spec[c, at, :]
+            a = jnp.dot(staged[c, at, :], forward[0], preferred_element_type=F32)
+            b = filt_spec[c, at, :]
             a_re, a_im, b_re, b_im = a[:, :INNER], a[:, INNER:], b[:, :INNER], b[:, INNER:]
             prod = jnp.concatenate([a_re * b_re - a_im * b_im, a_re * b_im + a_im * b_re], axis=1)
-            mixed[at, :] = both(prod.astype(BF), inverse)
+            mixed[at, :] = jnp.dot(prod.astype(BF), inverse[0], preferred_element_type=F32)
         data = []
         for f in range(OUTER):
             cos, sin = twiddle[0, pl.ds(f, 1), :], twiddle[1, pl.ds(f, 1), :]

time: 62 us -> 62 us (level)
  no operation moved by 1% of the time
where the time goes in v5:
time: 62 us; the launch traced here: 61.9 us
  Pallas kernels  61.2 us (99%)
  local copies, waits for them, and re-layouts  0.71 us (1%)
    pallas_call x1, Pallas kernels, on_device(): pl.pallas_call(functools.partial(kernel, depth=depth, tp_count=tp_count,...  61.2 us

profile of v5, /device:TPU:1, one launch (start us, length us, event | category | flops | bytes accessed | tf_op | source)
XLA Modules:
  0.0 61.9 jit_solution(6215501712153891127)
XLA Ops:
  0.0 61.2 %hyena.1 = bf16[32,4096]{1,0:T(8,128)(2,1)S(1)} custom-call(bf16[256,1024]{1,0:T(8,128)(2,1)} %act_hbm.1, bf16[1024,12288]{1,0:T(8,128)(2,1)} %weight.1, f32[32,4096]{1,0:T(8,128)} %bitcast.3, s32[4096]{0:T(1024)} %blocks_hbm.1, f32[4096]{0:T(1024)} %gains_hbm.1, bf16[2,256,256]{2,1,0:T(8,128)(2,1)} %constant.6.clone.forward_hbm, ...), custom_call_target="tpu_custom_call" | custom-call | tf_op jit(solution)/shard_map/hyena/pallas_call | solution.py:603
  61.2 0.7 %copy.10 = bf16[4096,32]{0,1:T(8,128)(2,1)} copy(bf16[4096,32]{0,1:T(8,128)(2,1)S(1)} %bitcast.2) | data formatting | bytes 524288
